TPU v7x, 512 devices: a whole 4x4x16 slice. The times are simulated.
512 devices in a mesh: leaf: 8 (over x, core), bulk: 64 (over y, z).
Axes of the slice: x: 4, y: 4, z: 16, core: 2. Of those that a mesh axis runs over, the one named last changes fastest.
Arguments:
- particles: float32 [16384, 4, 512], P(('leaf', 'bulk')), may hold values from -6 to 6
- velocities: float32 [16384, 3, 512], P(('leaf', 'bulk')), may hold values from -6 to 6
- cell_table: float32 [10, 131072], P(None, ('leaf', 'bulk')), may hold values from -8 to 8
- top_cells: float32 [10, 512], P(None, 'leaf'), may hold values from -12 to 12
- active_ids: int32 [2048], P(('leaf', 'bulk')), may hold values from 0 to 31, as said below
- active_count: int32 [512], P(('leaf', 'bulk')), may hold values from 1 to 4, as said below
- cell_requests: int32 [512, 64, 16], P(('leaf', 'bulk')), may hold values from -1 to 255, as said below
- cell_lists: int32 [2048, 64], P(('leaf', 'bulk')), may hold values from 0 to 1023, as said below
- leaf_requests: int32 [512, 64, 2], P(('leaf', 'bulk')), may hold values from -1 to 31, as said below
- leaf_lists: int32 [2048, 6], P(('leaf', 'bulk')), may hold values from 0 to 127, as said below
- targets: int32 [16384], P(('leaf', 'bulk')), may hold values from 0 to 63, as said below
Outputs:
- moved_particles: float32 [16384, 4, 512], P(('leaf', 'bulk'))
- moved_velocities: float32 [16384, 3, 512], P(('leaf', 'bulk'))
Inputs may be any that keep to these rules, and one draw needn't show every extreme that they name: `active_ids`: one device's 4 entries are distinct buckets of that device; only its first active_count entries are active. `active_count`: some device has 4 in every draw. `cell_requests`: entry [r, p, k] names a cell of bulk index p of r's leaf group, or is -1 for an unused slot; in each row [r, p] the used entries come first, are distinct and number 8 or more; in every draw one bulk index of each leaf group receives 16 from every device of it. `cell_lists`: entry f names slot f mod 16 of bulk peer f // 16 in its device's row of cell_requests, always a used one; one slot's entries are distinct. `leaf_requests`: entry [r, p, k] names a bucket of bulk index p of r's leaf group, or is -1 for an unused slot; no device asks its own bulk index; for every other peer the used entries come first, are distinct and number 1 or more; in every draw one bulk index of each leaf group receives 2 from every other device of it. `leaf_lists`: entry f names slot f mod 2 of bulk peer f // 2 in its device's row of leaf_requests, always a used one; one slot's entries are distinct. `targets`: within one leaf group, bucket j of the device with bulk index s goes to bulk index (s + t) mod 64, where the shift t depends only on the group and j; each device sends exactly 2 buckets to each of 16 bulk indices; the shifts 1 and 32 are among those of every group.
All inputs are finite; a program needn't handle non-finite values.
Results may differ from a plain program's by a relative error of at most 0.0003.
Values sent between devices are 32-bit elements; how exact they have to be, the bound alone decides.
A program may use at most 64 MiB of HBM per device.

v0:
```python
import jax
import jax.numpy as jnp
from jax import lax
from jax.sharding import PartitionSpec as P

step_time = 0.5
pair_soft = 0.01
cell_soft = 1.0


def cell_pull(points, moments):
    sep_x = points[0][:, None] - moments[1][None, :]
    sep_y = points[1][:, None] - moments[2][None, :]
    sep_z = points[2][:, None] - moments[3][None, :]
    inv_one = lax.rsqrt(sep_x * sep_x + sep_y * sep_y + sep_z * sep_z + cell_soft)
    inv_two = inv_one * inv_one
    inv_three = inv_two * inv_one
    inv_five = inv_three * inv_two
    tensor_x = moments[4] * sep_x + moments[7] * sep_y + moments[8] * sep_z
    tensor_y = moments[7] * sep_x + moments[5] * sep_y + moments[9] * sep_z
    tensor_z = moments[8] * sep_x + moments[9] * sep_y + moments[6] * sep_z
    quadric = sep_x * tensor_x + sep_y * tensor_y + sep_z * tensor_z
    radial = -moments[0] * inv_three - 2.5 * quadric * inv_five * inv_two
    pull_x = jnp.sum(radial * sep_x + tensor_x * inv_five, axis=1)
    pull_y = jnp.sum(radial * sep_y + tensor_y * inv_five, axis=1)
    pull_z = jnp.sum(radial * sep_z + tensor_z * inv_five, axis=1)
    return jnp.stack([pull_x, pull_y, pull_z])


def pair_pull(points, sources):
    pair_scale = 1.0 / sources.shape[1]
    sep_x = sources[0][None, :] - points[0][:, None]
    sep_y = sources[1][None, :] - points[1][:, None]
    sep_z = sources[2][None, :] - points[2][:, None]
    inv_one = lax.rsqrt(sep_x * sep_x + sep_y * sep_y + sep_z * sep_z + pair_soft)
    weighted = (sources[3] * pair_scale)[None, :] * inv_one * inv_one * inv_one
    return jnp.stack(
        [
            jnp.sum(weighted * sep_x, axis=1),
            jnp.sum(weighted * sep_y, axis=1),
            jnp.sum(weighted * sep_z, axis=1),
        ]
    )


def to_slots(state, source_ids):
    safe_ids = jnp.maximum(source_ids, 0)
    picked = jnp.take(state, safe_ids.reshape(-1), axis=0)
    picked = picked.reshape(source_ids.shape + state.shape[1:])
    keep_mask = (source_ids >= 0).reshape(source_ids.shape + (1,) * (state.ndim - 1))
    return jnp.where(keep_mask, picked, jnp.zeros_like(picked))


def on_device(
    particles,
    velocities,
    cell_table,
    top_cells,
    active_ids,
    active_count,
    cell_requests,
    cell_lists,
    leaf_requests,
    leaf_lists,
    targets,
):
    peer_count = lax.axis_size("bulk")
    own_index = lax.axis_index("bulk")
    buck_dev = particles.shape[0]
    per_peer = max(2, buck_dev // peer_count)
    shifts = jnp.mod(targets - own_index, peer_count)
    order_ids = jnp.arange(buck_dev, dtype=jnp.int32)
    same_shift = (shifts[:, None] == shifts[None, :]) & (order_ids[None, :] < order_ids[:, None])
    slot_ranks = jnp.sum(same_shift.astype(jnp.int32), axis=1)
    slot_table = (
        jnp.full((peer_count, per_peer), -1, jnp.int32).at[shifts, slot_ranks].set(order_ids)
    )
    send_ids = slot_table[jnp.mod(jnp.arange(peer_count, dtype=jnp.int32) - own_index, peer_count)]
    arrive_at = jnp.mod(own_index - shifts, peer_count) * per_peer + slot_ranks

    def place_arrived(received):
        return jnp.take(received.reshape((-1,) + received.shape[2:]), arrive_at, axis=0)

    asked_cells = lax.all_to_all(cell_requests[0], "bulk", split_axis=0, concat_axis=0, tiled=True)
    asked_leaves = lax.all_to_all(leaf_requests[0], "bulk", split_axis=0, concat_axis=0, tiled=True)
    cell_rows = to_slots(cell_table.T, asked_cells)
    leaf_rows = to_slots(particles, asked_leaves)
    own_buckets = jnp.take(particles, active_ids, axis=0)
    act_points = own_buckets[:, :3]
    shard_piece = lax.all_gather(top_cells, "leaf", axis=1, tiled=True)
    far_pull = lax.map(lambda points: cell_pull(points, shard_piece), act_points)
    got_cells = lax.all_to_all(cell_rows, "bulk", split_axis=0, concat_axis=0, tiled=True)
    got_leaves = lax.all_to_all(leaf_rows, "bulk", split_axis=0, concat_axis=0, tiled=True)
    fetched_cells = got_cells.reshape(-1, got_cells.shape[2]).T
    fetched_leaves = got_leaves.reshape((-1,) + got_leaves.shape[2:])

    def near_pull(inputs):
        own_bucket, cell_picks, leaf_picks = inputs
        chosen = jnp.take(fetched_cells, cell_picks, axis=1)
        sources = jnp.concatenate(
            [own_bucket[None], jnp.take(fetched_leaves, leaf_picks, axis=0)], axis=0
        )
        flat_sources = jnp.transpose(sources, (1, 0, 2)).reshape(sources.shape[1], -1)
        return cell_pull(own_bucket[:3], chosen) + pair_pull(own_bucket[:3], flat_sources)

    pulls_total = far_pull + lax.map(near_pull, (own_buckets, cell_lists, leaf_lists))
    alive_mask = (jnp.arange(active_ids.shape[0], dtype=jnp.int32) < active_count[0]).astype(
        jnp.float32
    )
    kick_terms = step_time * pulls_total * alive_mask[:, None, None]
    new_speed = velocities.at[active_ids].add(kick_terms)
    new_place = particles[:, :3] + step_time * new_speed
    new_state = jnp.concatenate([new_place, particles[:, 3:]], axis=1)
    return (
        place_arrived(
            lax.all_to_all(
                to_slots(new_state, send_ids), "bulk", split_axis=0, concat_axis=0, tiled=True
            )
        ),
        place_arrived(
            lax.all_to_all(
                to_slots(new_speed, send_ids), "bulk", split_axis=0, concat_axis=0, tiled=True
            )
        ),
    )


def solution(mesh):
    placed = (
        P(("leaf", "bulk"), None, None),
        P(("leaf", "bulk"), None, None),
        P(None, ("leaf", "bulk")),
        P(None, "leaf"),
        P(("leaf", "bulk")),
        P(("leaf", "bulk")),
        P(("leaf", "bulk"), None, None),
        P(("leaf", "bulk"), None),
        P(("leaf", "bulk"), None, None),
        P(("leaf", "bulk"), None),
        P(("leaf", "bulk")),
    )
    return jax.shard_map(
        on_device,
        mesh=mesh,
        in_specs=placed,
        out_specs=(P(("leaf", "bulk"), None, None), P(("leaf", "bulk"), None, None)),
        check_vma=False,
    )
```

profile of v0, /device:TPU:6, one launch (start us, length us, event | category | flops | bytes accessed | tf_op | source)
XLA Modules:
  0.0 299.2 jit_solution(13765534313157201365)
XLA Ops:
  0.7 1.4 copy.83
  2.0 18.7 %all-to-all-start.2 = ((s32[64,1,2]{2,1,0:T(1,128)}), s32[64,1,2]{2,1,0:T(1,128)S(1)}, u32[]{:S(2)}, u32[]{:S(2)}) async-start(s32[64,1,2]{2,1,0:T(1,128)} %copy.83), calls=%async_computation.2 | async-start | bytes 65536 | tf_op jit(solution)/shard_map/all_to_all | solution.py:85
  22.1 13.0 %all-gather = f32[8,64,10]{1,2,0:T(8,128)S(1)} all-gather(f32[1,64,10]{1,2,0:T(8,128)} %bitcast.197), channel_id=1, replica_groups=mesh['leaf'=8,'bulk'=64] {'leaf'}, dimensions={0}, use_global_device_ids=true | all-gather | bytes 23040 | tf_op jit(solution)/shard_map/all_gather | solution.py:90
  36.8 2.0 scatter_fusion
  41.1 15.1 %all-to-all-start = ((s32[64,1,16]{2,1,0:T(1,128)}), s32[64,1,16]{2,1,0:T(1,128)S(1)}, u32[]{:S(2)}, u32[]{:S(2)}) async-start(s32[64,1,16]{2,1,0:T(1,128)} %bitcast.41), calls=%async_computation | async-start | bytes 65536 | tf_op jit(solution)/shard_map/all_to_all | solution.py:84
  56.6 1.2 gather_fusion.8
  58.3 12.3 %all-to-all-done = s32[64,1,16]{2,1,0:T(1,128)S(1)} async-done(((s32[64,1,16]{2,1,0:T(1,128)}), s32[64,1,16]{2,1,0:T(1,128)S(1)}, u32[]{:S(2)}, u32[]{:S(2)}) %all-to-all-start) | async-done | bytes 4128 | tf_op jit(solution)/shard_map/all_to_all | solution.py:84
  71.1 2.8 gather_fusion.4
  75.3 4.6 %all-to-all-start.1 = ((f32[64,1,160]{2,1,0:T(1,128)}), f32[64,1,160]{2,1,0:T(1,128)S(1)}, u32[]{:S(2)}, u32[]{:S(2)}) async-start(f32[64,1,160]{2,1,0:T(1,128)} %reshape.519), calls=%async_computation.1 | async-start | bytes 131072 | tf_op jit(solution)/shard_map/all_to_all | solution.py:92
  79.9 1.3 broadcast_select_fusion.4
  81.2 13.5 %all-to-all-done.1 = f32[64,1,160]{2,1,0:T(1,128)S(1)} async-done(((f32[64,1,160]{2,1,0:T(1,128)}), f32[64,1,160]{2,1,0:T(1,128)S(1)}, u32[]{:S(2)}, u32[]{:S(2)}) %all-to-all-start.1) | async-done | bytes 40992 | tf_op jit(solution)/shard_map/all_to_all | solution.py:92
  94.7 4.8 %all-to-all-start.3 = ((f32[64,2,4,512]{3,2,1,0:T(4,128)}), f32[64,2,4,512]{3,2,1,0:T(4,128)S(1)}, u32[]{:S(2)}, u32[]{:S(2)}) async-start(f32[64,2,4,512]{3,2,1,0:T(4,128)} %broadcast_select_fusion.4), calls=%async_computation.3 | async-start | bytes 2097152 | tf_op jit(solution)/shard_map/all_to_all | solution.py:93
  100.3 9.5 %while.21 = (s32[]{:T(128)}, f32[4,3,512]{2,1,0:T(4,128)S(1)}, f32[1,512]{1,0:T(1,128)S(1)}, f32[4,3,512]{2,1,0:T(4,128)S(1)}, f32[10,512]{1,0:T(8,128)S(1)}, /*index=5*/s32[]{:T(128)}, s32[]{:T(128)}, s32[]{}, s32[]{}) while((s32[]{:T(128)}, f32[4,3,512]{2,1,0:T(4,128)S(1)}, f32[1,512]{1,0:T(1,128)S(1)}, f32[4,3,512]{2,1,0:T(4,128)S(1)}, ...), condition=%wide.region_6.7_spmd, body=%wide.region_2.6_spmd.sunk | while | flops 12846596 | bytes 96389 | solution.py:91
  100.3 2.3 fusion.86
  102.7 2.3 fusion.86
  105.1 2.3 fusion.86
  107.5 2.3 fusion.86
  111.4 40.3 %all-to-all-done.3 = f32[64,2,4,512]{3,2,1,0:T(4,128)S(1)} async-done(((f32[64,2,4,512]{3,2,1,0:T(4,128)}), f32[64,2,4,512]{3,2,1,0:T(4,128)S(1)}, u32[]{:S(2)}, u32[]{:S(2)}) %all-to-all-start.3) | async-done | bytes 1048608 | tf_op jit(solution)/shard_map/all_to_all | solution.py:93
  151.8 33.6 %while.22 = (s32[]{:T(128)}, f32[4,3,512]{2,1,0:T(4,128)S(1)}, s32[4,64]{1,0:T(4,128)S(1)}, f32[10,1024]{0,1:T(8,128)S(1)}, f32[4,4,512]{2,1,0:T(4,128)S(1)}, /*...) while((s32[]{:T(128)}, f32[4,3,512]{2,1,0:T(4,128)S(1)}, ...), condition=%wide.region_14.16_spmd, body=%wide.region_7.15_spmd.sunk | while | flops 34673976 | bytes 699565 | solution.py:106
  152.8 5.9 %fusion.93 = (f32[512]{0:T(512)S(1)}, f32[512]{0:T(512)S(1)}, f32[512]{0:T(512)S(1)}) fusion(f32[512]{0:T(512)S(1)} %bitcast.170, f32[3584]{0:T(1024)S(1)} %sub.1002, f32[512]{0:T(512)S(1)} %bitcast.172, f32[3584]{0:T(1024)S(1)} %sub.1003, f32[512]{0:T(512)S(1)} %bitcast.174, f32[3584]{0:T(1024)S(1)} %sub.1004, f32[3584]{0:T(1024)S(1)} %mul.1508), kind=kLoop, calls=%fused_computation.74.clone.1 | loop fusion | flops 33028608 | bytes 69632 | tf_op jit(solution)/shard_map/while/body/eval_jaxpr/reduce_sum | solution.py:39
  161.2 5.9 %fusion.93 = (f32[512]{0:T(512)S(1)}, f32[512]{0:T(512)S(1)}, f32[512]{0:T(512)S(1)}) fusion(f32[512]{0:T(512)S(1)} %bitcast.170, f32[3584]{0:T(1024)S(1)} %sub.1002, f32[512]{0:T(512)S(1)} %bitcast.172, f32[3584]{0:T(1024)S(1)} %sub.1003, f32[512]{0:T(512)S(1)} %bitcast.174, f32[3584]{0:T(1024)S(1)} %sub.1004, f32[3584]{0:T(1024)S(1)} %mul.1508), kind=kLoop, calls=%fused_computation.74.clone.1 | loop fusion | flops 33028608 | bytes 69632 | tf_op jit(solution)/shard_map/while/body/eval_jaxpr/reduce_sum | solution.py:39
  169.6 5.9 %fusion.93 = (f32[512]{0:T(512)S(1)}, f32[512]{0:T(512)S(1)}, f32[512]{0:T(512)S(1)}) fusion(f32[512]{0:T(512)S(1)} %bitcast.170, f32[3584]{0:T(1024)S(1)} %sub.1002, f32[512]{0:T(512)S(1)} %bitcast.172, f32[3584]{0:T(1024)S(1)} %sub.1003, f32[512]{0:T(512)S(1)} %bitcast.174, f32[3584]{0:T(1024)S(1)} %sub.1004, f32[3584]{0:T(1024)S(1)} %mul.1508), kind=kLoop, calls=%fused_computation.74.clone.1 | loop fusion | flops 33028608 | bytes 69632 | tf_op jit(solution)/shard_map/while/body/eval_jaxpr/reduce_sum | solution.py:39
  178.0 5.9 %fusion.93 = (f32[512]{0:T(512)S(1)}, f32[512]{0:T(512)S(1)}, f32[512]{0:T(512)S(1)}) fusion(f32[512]{0:T(512)S(1)} %bitcast.170, f32[3584]{0:T(1024)S(1)} %sub.1002, f32[512]{0:T(512)S(1)} %bitcast.172, f32[3584]{0:T(1024)S(1)} %sub.1003, f32[512]{0:T(512)S(1)} %bitcast.174, f32[3584]{0:T(1024)S(1)} %sub.1004, f32[3584]{0:T(1024)S(1)} %mul.1508), kind=kLoop, calls=%fused_computation.74.clone.1 | loop fusion | flops 33028608 | bytes 69632 | tf_op jit(solution)/shard_map/while/body/eval_jaxpr/reduce_sum | solution.py:39
  186.5 1.2 gather_fusion.6
  187.7 1.5 fusion.63
  189.2 6.4 %all-to-all-start.5 = ((f32[64,2,3,512]{3,1,2,0:T(2,128)}), f32[64,2,3,512]{3,1,2,0:T(2,128)S(1)}, u32[]{:S(2)}, u32[]{:S(2)}) async-start(f32[64,2,3,512]{3,1,2,0:T(2,128)} %fusion.63), calls=%async_computation.5 | async-start | bytes 1572864 | tf_op jit(solution)/shard_map/all_to_all | solution.py:121
  196.0 1.2 gather_fusion.9
  197.5 1.3 broadcast_select_fusion.3
  198.8 37.9 %all-to-all-done.5 = f32[64,2,3,512]{3,1,2,0:T(2,128)S(1)} async-done(((f32[64,2,3,512]{3,1,2,0:T(2,128)}), f32[64,2,3,512]{3,1,2,0:T(2,128)S(1)}, u32[]{:S(2)}, u32[]{:S(2)}) %all-to-all-start.5) | async-done | bytes 786464 | tf_op jit(solution)/shard_map/all_to_all | solution.py:121
  236.7 7.3 %all-to-all-start.4 = ((f32[64,2,4,512]{3,2,1,0:T(4,128)}), f32[64,2,4,512]{3,2,1,0:T(4,128)}, u32[]{:S(2)}, u32[]{:S(2)}) async-start(f32[64,2,4,512]{3,2,1,0:T(4,128)} %broadcast_select_fusion.3), calls=%async_computation.4 | async-start | bytes 2097152 | tf_op jit(solution)/shard_map/all_to_all | solution.py:116
  245.9 50.5 %all-to-all-done.4 = f32[64,2,4,512]{3,2,1,0:T(4,128)} async-done(((f32[64,2,4,512]{3,2,1,0:T(4,128)}), f32[64,2,4,512]{3,2,1,0:T(4,128)}, u32[]{:S(2)}, u32[]{:S(2)}) %all-to-all-start.4) | async-done | bytes 1048608 | tf_op jit(solution)/shard_map/all_to_all | solution.py:116
  296.5 1.9 gather_fusion.5
  (179 shorter events, 23.8 us)
Async XLA Ops:
  0.6 39.0 %copy-start.3 = (s32[1,64,16]{1,2,0:T(8,128)S(1)}, s32[1,64,16]{1,2,0:T(8,128)}, u32[]{:S(2)}) copy-start(s32[1,64,16]{1,2,0:T(8,128)} %param.23) | copy-start | bytes 12292
  0.6 39.7 %copy-start.2 = (f32[10,256]{1,0:T(8,128)S(1)}, f32[10,256]{1,0:T(8,128)}, u32[]{:S(2)}) copy-start(f32[10,256]{1,0:T(8,128)} %param.19) | copy-start | bytes 30724
  2.0 39.1 %all-to-all-start.2 = ((s32[64,1,2]{2,1,0:T(1,128)}), s32[64,1,2]{2,1,0:T(1,128)S(1)}, u32[]{:S(2)}, u32[]{:S(2)}) async-start(s32[64,1,2]{2,1,0:T(1,128)} %copy.83), calls=%async_computation.2 | async-start | bytes 65536 | tf_op jit(solution)/shard_map/all_to_all | solution.py:85
  35.1 21.5 %copy-start = (f32[32,4,512]{2,1,0:T(4,128)S(1)}, f32[32,4,512]{2,1,0:T(4,128)}, u32[]{:S(2)}) copy-start(f32[32,4,512]{2,1,0:T(4,128)} %param.17) | copy-start | bytes 786436
  41.1 29.5 %all-to-all-start = ((s32[64,1,16]{2,1,0:T(1,128)}), s32[64,1,16]{2,1,0:T(1,128)S(1)}, u32[]{:S(2)}, u32[]{:S(2)}) async-start(s32[64,1,16]{2,1,0:T(1,128)} %bitcast.41), calls=%async_computation | async-start | bytes 65536 | tf_op jit(solution)/shard_map/all_to_all | solution.py:84
  75.3 19.4 %all-to-all-start.1 = ((f32[64,1,160]{2,1,0:T(1,128)}), f32[64,1,160]{2,1,0:T(1,128)S(1)}, u32[]{:S(2)}, u32[]{:S(2)}) async-start(f32[64,1,160]{2,1,0:T(1,128)} %reshape.519), calls=%async_computation.1 | async-start | bytes 131072 | tf_op jit(solution)/shard_map/all_to_all | solution.py:92
  94.7 57.1 %all-to-all-start.3 = ((f32[64,2,4,512]{3,2,1,0:T(4,128)}), f32[64,2,4,512]{3,2,1,0:T(4,128)S(1)}, u32[]{:S(2)}, u32[]{:S(2)}) async-start(f32[64,2,4,512]{3,2,1,0:T(4,128)} %broadcast_select_fusion.4), calls=%async_computation.3 | async-start | bytes 2097152 | tf_op jit(solution)/shard_map/all_to_all | solution.py:93
  100.2 51.5 %copy-start.5 = (s32[4,64]{1,0:T(4,128)S(1)}, s32[4,64]{1,0:T(4,128)}, u32[]{:S(2)}) copy-start(s32[4,64]{1,0:T(4,128)} %param.24) | copy-start | bytes 3076
  100.2 51.5 %copy-start.6 = (s32[4,6]{1,0:T(4,128)S(1)}, s32[4,6]{1,0:T(4,128)}, u32[]{:S(2)}) copy-start(s32[4,6]{1,0:T(4,128)} %param.26) | copy-start | bytes 292
  151.8 33.7 %copy-start.1 = (f32[32,3,512]{2,0,1:T(8,128)S(1)}, f32[32,3,512]{2,0,1:T(8,128)}, u32[]{:S(2)}) copy-start(f32[32,3,512]{2,0,1:T(8,128)} %param.18) | copy-start | bytes 589828
  189.2 47.5 %all-to-all-start.5 = ((f32[64,2,3,512]{3,1,2,0:T(2,128)}), f32[64,2,3,512]{3,1,2,0:T(2,128)S(1)}, u32[]{:S(2)}, u32[]{:S(2)}) async-start(f32[64,2,3,512]{3,1,2,0:T(2,128)} %fusion.63), calls=%async_computation.5 | async-start | bytes 1572864 | tf_op jit(solution)/shard_map/all_to_all | solution.py:121
  198.8 45.2 %copy-start.4 = (s32[32]{0:T(128)S(1)}, s32[32]{0:T(128)}, u32[]{:S(2)}) copy-start(s32[32]{0:T(128)} %param.27) | copy-start | bytes 388
  236.7 59.8 %all-to-all-start.4 = ((f32[64,2,4,512]{3,2,1,0:T(4,128)}), f32[64,2,4,512]{3,2,1,0:T(4,128)}, u32[]{:S(2)}, u32[]{:S(2)}) async-start(f32[64,2,4,512]{3,2,1,0:T(4,128)} %broadcast_select_fusion.3), calls=%async_computation.4 | async-start | bytes 2097152 | tf_op jit(solution)/shard_map/all_to_all | solution.py:116
where the time goes:
time: 300 us; the launch traced here: 299 us
  waiting for transfers between devices  154 us (51%)
  starting transfers between devices  57 us (19%)
  other arithmetic  48.6 us (16%)
  local copies, waits for them, and re-layouts  23.8 us (8%)
  blocking collectives  13 us (4%)
    all_to_all x1, waiting for transfers between devices, on_device(): lax.all_to_all(to_slots(new_state, send_ids), 'bulk', split_axis=0, conca...  50.5 us
    all_to_all x1, waiting for transfers between devices, on_device(): lax.all_to_all(leaf_rows, 'bulk', split_axis=0, concat_axis=0, tiled=True)  40.3 us
    all_to_all x1, waiting for transfers between devices, on_device(): lax.all_to_all(to_slots(new_speed, send_ids), 'bulk', split_axis=0, conca...  37.9 us
    reduce_sum x4, other arithmetic, pair_pull(): jnp.sum(weighted * sep_x, axis=1)  23.6 us
    all_to_all x1, starting transfers between devices, on_device(): lax.all_to_all(leaf_requests[0], 'bulk', split_axis=0, concat_axis=0, til...  18.7 us
    all_to_all x1, starting transfers between devices, on_device(): lax.all_to_all(cell_requests[0], 'bulk', split_axis=0, concat_axis=0, til...  15.1 us
    all_to_all x1, waiting for transfers between devices, on_device(): lax.all_to_all(cell_rows, 'bulk', split_axis=0, concat_axis=0, tiled=True)  13.5 us
    all_gather x1, blocking collectives, on_device(): shard_piece = lax.all_gather(top_cells, 'leaf', axis=1, tiled=True)  13 us
  transfers between devices with their start and end apart: 6, of which 5 were waited for; matrix products, arithmetic and copies ran while one was open for 9% of the time, Pallas kernels for 0%

commit v1 on v0

v1 whole, which is shorter than its diff:
```python
import functools

import jax
import jax.numpy as jnp
from jax import lax
from jax.experimental import pallas as pl
from jax.experimental.pallas import tpu as pltpu
from jax.sharding import PartitionSpec as P

MESH = pl.DeviceIdType.MESH
step_time = 0.5
pair_soft = 0.01
cell_soft = 1.0

NY, NZ, NL = 4, 16, 8
NB = 32
ACT = 4
LPER = 6
CPER = 64
SUBS = 4
SROW = NB // SUBS
OCT = 64


def pair_terms(px, py, pz, src, accs):
    ax, ay, az = accs
    for sx, sy, sz, sm in src:
        dx = sx - px
        dy = sy - py
        dz = sz - pz
        inv = lax.rsqrt(dx * dx + dy * dy + (dz * dz + pair_soft))
        w = sm * inv * (inv * inv)
        ax = ax + w * dx
        ay = ay + w * dy
        az = az + w * dz
    return ax, ay, az


def cell_terms(px, py, pz, cells, accs):
    ax, ay, az = accs
    for m, cx, cy, cz, xx, yy, zz, xy, xz, yz in cells:
        dx = px - cx
        dy = py - cy
        dz = pz - cz
        inv = lax.rsqrt(dx * dx + dy * dy + (dz * dz + cell_soft))
        inv2 = inv * inv
        inv3 = inv2 * inv
        inv5 = inv3 * inv2
        tx = xx * dx + xy * dy + xz * dz
        ty = xy * dx + yy * dy + yz * dz
        tz = xz * dx + yz * dy + zz * dz
        u = dx * tx + dy * ty + dz * tz
        rad = m * inv3 + (2.5 * u) * (inv5 * inv2)
        ax = ax + (tx * inv5 - rad * dx)
        ay = ay + (ty * inv5 - rad * dy)
        az = az + (tz * inv5 - rad * dz)
    return ax, ay, az


def kernel(
    part, vel, cells, top, act_ids, act_cnt, cell_lists, cell_req, leaf_req, leaf_lists, targets,
    outp, outv,
    p_all, v_all, v_y, c_all, t_all, top_m, codes_v, codes_s, l_send,
    l0, l1, l2, l3, k0, k1, k2, k3, p_rec, pts, acc, own, chosen, picks, near,
    p_ss, p_rs, c_ss, c_rs, v_ss, v_rs, t_ss, t_rs, d_ss, d_rs, vy_ss, vy_rs,
    cy_ss, cy_rs, l_ss, l_rs, pr_ss, pr_rs, kz_ss, kz_rs, ky_ss, ky_rs, loc,
):
    l_rec = (l0, l1, l2, l3)
    k_all = (k0, k1, k2, k3)
    leaf = lax.axis_index("leaf")
    bulk = lax.axis_index("bulk")
    y = bulk // NZ
    z = bulk % NZ

    def row_peer(d):
        return y * NZ + (z + d) % NZ

    def col_peer(d):
        return ((y + d) % NY) * NZ + z

    own_p = pltpu.make_async_copy(part, p_all.at[z], loc.at[0])
    own_v = pltpu.make_async_copy(vel, v_y.at[y], loc.at[1])
    own_c = pltpu.make_async_copy(cells, c_all.at[bulk], loc.at[2])
    own_t = pltpu.make_async_copy(top, t_all.at[leaf], loc.at[3])
    own_p.start()
    own_v.start()
    own_c.start()
    own_t.start()

    def code_of(a, e):
        f = leaf_lists[a, e]
        peer = f // LCAP
        return peer * NB + leaf_req[f % LCAP, peer]

    LCAP = 2
    rows = lax.broadcasted_iota(jnp.int32, (8, 128), 0)
    lanes = lax.broadcasted_iota(jnp.int32, (8, 128), 1)
    code = jnp.zeros((8, 128), jnp.int32)
    for a in range(ACT):
        for e in range(LPER):
            code = jnp.where((rows == a) & (lanes == e), code_of(a, e), code)
    codes_v[y] = code

    barrier = pltpu.get_barrier_semaphore()

    def greet(dev):
        pl.semaphore_signal(barrier, inc=1, device_id=dev, device_id_type=MESH)

    for d in range(1, NZ):
        greet({"bulk": row_peer(d)})
    for d in range(1, NY):
        greet({"bulk": col_peer(d)})
    for d in range(1, NL):
        greet({"leaf": (leaf + d) % NL})
    pl.semaphore_wait(barrier, NZ + NY + NL - 3)

    def remote(src, dst, ss, rs, dev):
        return pltpu.make_async_remote_copy(
            src_ref=src, dst_ref=dst, send_sem=ss, recv_sem=rs, device_id=dev, device_id_type=MESH
        )

    def ring_dev(way):
        return {"bulk": row_peer(1 if way == 0 else NZ - 1)}

    def ring_src(way, h):
        return (z + NZ - h) % NZ if way == 0 else (z + h) % NZ

    def p_copy(way, h, sub, first=False):
        at = ring_src(way, h)
        cut = pl.ds(sub * SROW, SROW)
        dst = p_all.at[at, cut]
        src = part.at[cut] if first else dst
        return remote(src, dst, p_ss.at[way, h, sub], p_rs.at[way, h, sub], ring_dev(way))

    def c_copy(way, h):
        at = c_all.at[y * NZ + ring_src(way, h)]
        src = cells if isinstance(h, int) and h == 0 else at
        return remote(src, at, c_ss.at[way, h], c_rs.at[way, h], ring_dev(way))

    def v_copy(way, h, sub):
        at = v_all.at[ring_src(way, h), sub]
        return remote(at, at, v_ss.at[way, h, sub], v_rs.at[way, h, sub], ring_dev(way))

    def t_copy(d):
        return remote(top, t_all.at[leaf], t_ss.at[d], t_rs.at[d], {"leaf": (leaf + d) % NL})

    def d_copy(d):
        return remote(
            codes_v.at[y], codes_v.at[y], d_ss.at[d], d_rs.at[d], {"bulk": col_peer(d)}
        )

    def vy_copy(d):
        return remote(vel, v_y.at[y], vy_ss.at[d], vy_rs.at[d], {"bulk": col_peer(d)})

    def cy_copy(d):
        blk = c_all.at[pl.ds(y * NZ, NZ)]
        return remote(blk, blk, cy_ss.at[d], cy_rs.at[d], {"bulk": col_peer(d)})

    def l_copy(a, d):
        return remote(
            l_send.at[d - 1, a], l_rec[a].at[y], l_ss.at[a, d], l_rs.at[a, d],
            {"bulk": col_peer(d)},
        )

    def pr_copy(d):
        return remote(
            p_rec.at[y], p_rec.at[y], pr_ss.at[d], pr_rs.at[d], {"bulk": col_peer(d)}
        )

    def kz_copy(a, d):
        at = k_all[a].at[y, z]
        return remote(at, at, kz_ss.at[a, d], kz_rs.at[a, d], {"bulk": row_peer(d)})

    def ky_copy(a, d):
        at = k_all[a].at[y]
        return remote(at, at, ky_ss.at[a, d], ky_rs.at[a, d], {"bulk": col_peer(d)})

    for d in range(1, NL):
        t_copy(d).start()
    for way in range(2):
        c_copy(way, 0).start()
    for d in range(1, NY):
        d_copy(d).start()
    for sub in range(SUBS):
        for way in range(2):
            p_copy(way, 0, sub, True).start()
    for d in range(1, NY):
        vy_copy(d).start()

    for a in range(ACT):
        bucket = part[act_ids[a]]
        own[a, pl.ds(0, 4), :] = bucket

        def spread(c, _, a=a):
            row = own[a, pl.ds(c, 1), :]
            pts[a, c] = jnp.transpose(jnp.broadcast_to(row, (128, 512)))
            return 0

        lax.fori_loop(0, 3, spread, 0)

    own_t.wait()
    for d in range(1, NL):
        t_copy(d).wait_recv()
    half = lax.broadcasted_iota(jnp.int32, (16, 128), 1) < 64
    for i in range(4):
        top_m[:, pl.ds(i * 128, 128)] = jnp.where(
            half, t_all[2 * i], pltpu.roll(t_all[2 * i + 1], 64, 1)
        )

    def src_rows(load, tiles=4):
        out = []
        for i in range(tiles):
            sx, sy, sz, sm = [load(c, pl.ds(i * 128, 128)) for c in range(4)]
            out.append((sx, sy, sz, sm * (1.0 / (512.0 * (LPER + 1)))))
        return out

    def self_top(a, o0, count):
        src = src_rows(lambda c, cut: own[a, pl.ds(c, 1), cut])

        def step(i, _):
            at = pl.ds(pl.multiple_of((o0 + i) * 8, 8), 8)
            px, py, pz = pts[a, 0, at, :], pts[a, 1, at, :], pts[a, 2, at, :]
            zero = jnp.zeros((8, 128), jnp.float32)
            accs = pair_terms(px, py, pz, src, (zero, zero, zero))
            tops = [
                [top_m[pl.ds(k, 1), pl.ds(j * 128, 128)] for k in range(10)] for j in range(4)
            ]
            accs = cell_terms(px, py, pz, tops, accs)
            for c in range(3):
                acc[a, c, at, :] = accs[c]
            return 0

        lax.fori_loop(0, count, step, 0)

    def near_part(a, o0, count):
        cut = pl.ds(pl.multiple_of((a // 2) * 128, 128), 128)
        lane = lax.broadcasted_iota(jnp.int32, (1, 128), 1)
        mine = (lane // CPER) == (a % 2)
        cell = [near[pl.ds(k, 1), cut] for k in range(10)]
        cell = [v if 1 <= k <= 3 else jnp.where(mine, v, 0.0) for k, v in enumerate(cell)]

        def step(i, _):
            at = pl.ds(pl.multiple_of((o0 + i) * 8, 8), 8)
            px, py, pz = pts[a, 0, at, :], pts[a, 1, at, :], pts[a, 2, at, :]
            accs = tuple(acc[a, c, at, :] for c in range(3))
            accs = cell_terms(px, py, pz, [cell], accs)
            for c in range(3):
                acc[a, c, at, :] = accs[c]
            return 0

        lax.fori_loop(0, count, step, 0)

    def p_event(i):
        h = i // SUBS
        sub = i % SUBS
        for way in range(2):
            mine = (sub < SUBS // 2) if way == 0 else (sub >= SUBS // 2)

            @pl.when((h < NZ // 2 - 1) | mine)
            def _():
                p_copy(way, h, sub).wait_recv()

            @pl.when((h < NZ // 2 - 2) | ((h == NZ // 2 - 2) & mine))
            def _():
                p_copy(way, h + 1, sub).start()

    def c_event(i):
        for way in range(2):
            if way == 0:
                c_copy(way, i).wait_recv()

                @pl.when(i < NZ // 2 - 1)
                def _():
                    c_copy(way, i + 1).start()
            else:

                @pl.when(i < NZ // 2 - 1)
                def _():
                    c_copy(way, i).wait_recv()

                @pl.when(i < NZ // 2 - 2)
                def _():
                    c_copy(way, i + 1).start()

    own_c.wait()

    def first_events(i, _):
        c_event(i)
        p_event(i)
        self_top(i // 8, (i % 8) * 8, 8)
        return 0

    lax.fori_loop(0, 8, first_events, 0)
    for d in range(1, NY):
        cy_copy(d).start()

    def more_events(i, _):
        p_event(i)
        self_top(i // 8, (i % 8) * 8, 8)
        return 0

    lax.fori_loop(8, 16, more_events, 0)

    own_v.wait()
    for d in range(1, NY):
        vy_copy(d).wait_recv()

    def pick_row(j, _):
        shift = (targets[j] - bulk) & 63
        to_z = (z + shift) & 15
        from_y = ((y * NZ + to_z - shift) & 63) >> 4
        for c in range(3):
            v_all[z, c, pl.ds(j, 1), :] = v_y[from_y, c, pl.ds(j, 1), :]
        return 0

    lax.fori_loop(0, NB, pick_row, 0)
    lax.fori_loop(16, 24, more_events, 0)

    for d in range(1, NY):
        cy_copy(d).wait_recv()

    def pick_cell(i, _):
        f = cell_lists[i // CPER, i % CPER]
        peer = f >> 4
        col = cell_req[f & 15, peer] & 255
        chosen[pl.ds(i, 1), :] = c_all[peer, pl.ds(col >> 3, 1), :]
        picks[pl.ds(i, 1), :] = jnp.full((1, 128), col & 7, jnp.int32)
        return 0

    lax.fori_loop(0, ACT * CPER, pick_cell, 0)
    got = chosen[...]
    group = picks[...]
    packed = jnp.where(group == 0, got, 0.0)
    for g in range(1, 8):
        packed = jnp.where(group == g, pltpu.roll(got, 128 - 16 * g, 1), packed)
    near[...] = jnp.transpose(packed)

    def last_events(i, _):
        p_event(i)
        self_top(i // 8, (i % 8) * 8, 8)
        return 0

    lax.fori_loop(24, 32, last_events, 0)

    own_p.wait()
    for d in range(1, NY):
        d_copy(d).wait_recv()
    codes_copy = pltpu.make_async_copy(codes_v, codes_s, loc.at[4])
    codes_copy.start()
    codes_copy.wait()

    def leaf_at(number):
        return p_all[(number >> 5) & 15, number & 31]

    for a in range(ACT):
        for d in range(1, NY):
            to_y = (y + d) % NY

            def fill(e, _, a=a, d=d, to_y=to_y):
                l_send[d - 1, a, e] = leaf_at(codes_s[to_y, a, e])
                return 0

            lax.fori_loop(0, LPER, fill, 0)
            l_copy(a, d).start()

        def fill_own(e, _, a=a):
            l_rec[a][y, e] = leaf_at(code_of(a, e))
            return 0

        lax.fori_loop(0, LPER, fill_own, 0)

    for way in range(2):
        for sub in range(3):
            v_copy(way, 0, sub).start()

    def pick_moved(j, _):
        from_z = (bulk - (targets[j] - bulk)) & 15
        p_rec[y, j] = p_all[from_z, j]
        return 0

    lax.fori_loop(0, NB, pick_moved, 0)
    for d in range(1, NY):
        pr_copy(d).start()

    for a in range(ACT):
        near_part(a, 0, OCT)

    def v_event(i):
        h = i // 3
        sub = i % 3
        for way in range(2):
            mine = (sub == 0) if way == 0 else (sub > 0)

            @pl.when((h < NZ // 2 - 1) | mine)
            def _():
                v_copy(way, h, sub).wait_recv()

            @pl.when((h < NZ // 2 - 2) | ((h == NZ // 2 - 2) & mine))
            def _():
                v_copy(way, h + 1, sub).start()

    def y_send(a):
        def wait_one(d, _):
            kz_copy(a, d).wait_recv()
            return 0

        lax.fori_loop(1, NZ, wait_one, 0)
        for d in range(1, NY):
            ky_copy(a, d).start()

    for a in range(ACT):
        for d in range(1, NY):
            l_copy(a, d).wait_recv()

        def block(e, _, a=a):
            from_y = (code_of(a, e) >> 9) & 3
            src = src_rows(lambda c, cut: l_rec[a][from_y, e, pl.ds(c, 1), cut])

            def step(i, _):
                at = pl.ds(pl.multiple_of(i * 8, 8), 8)
                px, py, pz = pts[a, 0, at, :], pts[a, 1, at, :], pts[a, 2, at, :]
                accs = tuple(acc[a, c, at, :] for c in range(3))
                accs = pair_terms(px, py, pz, src, accs)
                for c in range(3):
                    acc[a, c, at, :] = accs[c]
                return 0

            lax.fori_loop(0, OCT, step, 0)

            @pl.when(e % 2 == 1)
            def _():
                v_event(a * 3 + e // 2)

            return 0

        lax.fori_loop(0, LPER, block, 0)
        alive = jnp.where(a < act_cnt[0], 1.0, 0.0)
        ident = jnp.where(a < act_cnt[0], act_ids[a], -1).astype(jnp.float32)
        for c in range(3):
            pull = jnp.sum(jnp.transpose(acc[a, c]), axis=0, keepdims=True)
            k_all[a][y, z, pl.ds(c, 1), :] = step_time * pull * alive
        k_all[a][y, z, pl.ds(3, 1), :] = jnp.full((1, 512), ident, jnp.float32)

        def send_one(d, _, a=a):
            kz_copy(a, d).start()
            return 0

        lax.fori_loop(1, NZ, send_one, 0)
        if a > 0:
            y_send(a - 1)

    def tail_events(i, _):
        v_event(i)
        return 0

    lax.fori_loop(12, 24, tail_events, 0)
    y_send(ACT - 1)
    for d in range(1, NY):
        pr_copy(d).wait_recv()
    for a in range(ACT):
        for d in range(1, NY):
            ky_copy(a, d).wait_recv()

    def place(j, _):
        source = (bulk - (targets[j] - bulk)) & 63
        from_y = source >> 4
        from_z = source & 15
        number = j.astype(jnp.float32)
        hits = [k_all[a][from_y, from_z, pl.ds(3, 1), :] == number for a in range(ACT)]
        for c in range(3):
            speed = v_all[from_z, c, pl.ds(j, 1), :]
            kick = jnp.zeros((1, 512), jnp.float32)
            for a in range(ACT):
                kick = kick + jnp.where(
                    hits[a], k_all[a][from_y, from_z, pl.ds(c, 1), :], 0.0
                )
            speed = speed + kick
            outv[c, pl.ds(j, 1), :] = speed
            outp[j, pl.ds(c, 1), :] = p_rec[from_y, j, pl.ds(c, 1), :] + step_time * speed
        outp[j, pl.ds(3, 1), :] = p_rec[from_y, j, pl.ds(3, 1), :]
        return 0

    lax.fori_loop(0, NB, place, 0)

    for d in range(1, NL):
        t_copy(d).wait_send()

    def p_sent(i, _):
        h = i // SUBS
        sub = i % SUBS
        for way in range(2):
            mine = (sub < SUBS // 2) if way == 0 else (sub >= SUBS // 2)

            @pl.when((h < NZ // 2 - 1) | mine)
            def _():
                p_copy(way, h, sub).wait_send()

        return 0

    lax.fori_loop(0, 32, p_sent, 0)

    def v_sent(i, _):
        h = i // 3
        sub = i % 3
        for way in range(2):
            mine = (sub == 0) if way == 0 else (sub > 0)

            @pl.when((h < NZ // 2 - 1) | mine)
            def _():
                v_copy(way, h, sub).wait_send()

        return 0

    lax.fori_loop(0, 24, v_sent, 0)
    for h in range(NZ // 2):
        c_copy(0, h).wait_send()
        if h < NZ // 2 - 1:
            c_copy(1, h).wait_send()
    for d in range(1, NY):
        d_copy(d).wait_send()
        vy_copy(d).wait_send()
        cy_copy(d).wait_send()
        pr_copy(d).wait_send()
        for a in range(ACT):
            l_copy(a, d).wait_send()
            ky_copy(a, d).wait_send()
    for a in range(ACT):

        def kz_sent(d, _, a=a):
            kz_copy(a, d).wait_send()
            return 0

        lax.fori_loop(1, NZ, kz_sent, 0)


def on_device(
    particles,
    velocities,
    cell_table,
    top_cells,
    active_ids,
    active_count,
    cell_requests,
    cell_lists,
    leaf_requests,
    leaf_lists,
    targets,
):
    speeds = jnp.transpose(velocities, (1, 0, 2))
    cells = jnp.pad(cell_table.T, ((0, 0), (0, 6))).reshape(32, 128)
    top = jnp.pad(top_cells, ((0, 6), (0, 64)))
    vmem = pl.BlockSpec(memory_space=pltpu.VMEM)
    smem = pl.BlockSpec(memory_space=pltpu.SMEM)
    f32 = jnp.float32
    dma = pltpu.SemaphoreType.DMA
    placed, moved = pl.pallas_call(
        kernel,
        out_shape=(
            jax.ShapeDtypeStruct((NB, 4, 512), f32),
            jax.ShapeDtypeStruct((3, NB, 512), f32),
        ),
        in_specs=[vmem] * 4 + [smem] * 7,
        out_specs=(vmem, vmem),
        scratch_shapes=[
            pltpu.VMEM((NZ, NB, 4, 512), f32),
            pltpu.VMEM((NZ, 3, NB, 512), f32),
            pltpu.VMEM((NY, 3, NB, 512), f32),
            pltpu.VMEM((NY * NZ, 32, 128), f32),
            pltpu.VMEM((NL, 16, 128), f32),
            pltpu.VMEM((16, 512), f32),
            pltpu.VMEM((NY, 8, 128), jnp.int32),
            pltpu.SMEM((NY, 8, 128), jnp.int32),
            pltpu.VMEM((NY - 1, ACT, LPER, 4, 512), f32),
        ]
        + [pltpu.VMEM((NY, LPER, 4, 512), f32)] * ACT
        + [pltpu.VMEM((NY, NZ, 4, 512), f32)] * ACT
        + [
            pltpu.VMEM((NY, NB, 4, 512), f32),
            pltpu.VMEM((ACT, 3, 512, 128), f32),
            pltpu.VMEM((ACT, 3, 512, 128), f32),
            pltpu.VMEM((ACT, 8, 512), f32),
            pltpu.VMEM((ACT * CPER, 128), f32),
            pltpu.VMEM((ACT * CPER, 128), jnp.int32),
            pltpu.VMEM((128, ACT * CPER), f32),
            dma((2, 8, SUBS)),
            dma((2, 8, SUBS)),
            dma((2, 8)),
            dma((2, 8)),
            dma((2, 8, 3)),
            dma((2, 8, 3)),
            dma((NL,)),
            dma((NL,)),
            dma((NY,)),
            dma((NY,)),
            dma((NY,)),
            dma((NY,)),
            dma((NY,)),
            dma((NY,)),
            dma((ACT, NY)),
            dma((ACT, NY)),
            dma((NY,)),
            dma((NY,)),
            dma((ACT, NZ)),
            dma((ACT, NZ)),
            dma((ACT, NY)),
            dma((ACT, NY)),
            dma((5,)),
        ],
        compiler_params=pltpu.CompilerParams(
            collective_id=0, has_side_effects=True, vmem_limit_bytes=56 * 1024 * 1024
        ),
    )(
        particles,
        speeds,
        cells,
        top,
        active_ids,
        active_count,
        cell_lists,
        cell_requests[0].T,
        leaf_requests[0].T,
        leaf_lists,
        targets,
    )
    return placed, jnp.transpose(moved, (1, 0, 2))


def solution(mesh):
    placed = (
        P(("leaf", "bulk"), None, None),
        P(("leaf", "bulk"), None, None),
        P(None, ("leaf", "bulk")),
        P(None, "leaf"),
        P(("leaf", "bulk")),
        P(("leaf", "bulk")),
        P(("leaf", "bulk"), None, None),
        P(("leaf", "bulk"), None),
        P(("leaf", "bulk"), None, None),
        P(("leaf", "bulk"), None),
        P(("leaf", "bulk")),
    )
    return jax.shard_map(
        on_device,
        mesh=mesh,
        in_specs=placed,
        out_specs=(P(("leaf", "bulk"), None, None), P(("leaf", "bulk"), None, None)),
        check_vma=False,
    )
```

time: 300 us -> 160 us (0.53)
  Pallas kernels: 0 us -> 155 us
  waiting for transfers between devices: 154 us -> 0 us
  starting transfers between devices: 57 us -> 0 us
  other arithmetic: 48.6 us -> 0 us
  local copies, waits for them, and re-layouts: 23.8 us -> 3.85 us
  blocking collectives: 13 us -> 0 us
    pallas_call x0 -> x1, Pallas kernels: none -> 155 us  [on_device(): pl.pallas_call(kernel, out_shape=(jax.ShapeDtypeStruct((NB, 4, 512), f32)...]
    all_to_all x6 -> x0, waiting for transfers between devices: 154 us -> none  [the longest x1 50.5 us: on_device(): lax.all_to_all(to_slots(new_state, send_ids), 'bulk', split_axis=0, conca...]
    all_to_all x6 -> x0, starting transfers between devices: 57 us -> none  [the longest x1 18.7 us: on_device(): lax.all_to_all(leaf_requests[0], 'bulk', split_axis=0, concat_axis=0, til...]
    reduce_sum x13 -> x0, other arithmetic: 34.4 us -> none  [the longest x4 23.6 us: pair_pull(): jnp.sum(weighted * sep_x, axis=1)]
    gather x16 -> x0, local copies, waits for them, and re-layouts: 14.9 us -> none  [the longest x4 6.36 us: to_slots(): picked = jnp.take(state, safe_ids.reshape(-1), axis=0)]
    all_gather x1 -> x0, blocking collectives: 13 us -> none  [on_device(): shard_piece = lax.all_gather(top_cells, 'leaf', axis=1, tiled=True)]
    select_n x30 -> x0, other arithmetic: 8.15 us -> none  [the longest x4 4.48 us: to_slots(): return jnp.where(keep_mask, picked, jnp.zeros_like(picked))]
  transfers between devices with their start and end apart: 6 -> 0, of which waited for: 5 -> 0; matrix products, arithmetic and copies ran while one was open for 9% -> 0% of each run, Pallas kernels for 0% -> 0%
where the time goes in v1:
time: 160 us
  Pallas kernels  155 us (97%)
  local copies, waits for them, and re-layouts  3.85 us (2%)
    pallas_call x1, Pallas kernels, on_device(): pl.pallas_call(kernel, out_shape=(jax.ShapeDtypeStruct((NB, 4, 512), f32)...  155 us

profile of v1, /device:TPU:6, one launch (start us, length us, event | category | flops | bytes accessed | tf_op | source)
XLA Modules:
  0.0 159.8 jit_solution(190281950352420031)
XLA Ops:
  0.6 0.0 copy-start.2
  0.6 0.0 copy-start.1
  1.3 0.0 copy-done.2
  1.3 0.6 pad.9.top
  1.9 0.0 copy-done.1
  1.9 0.1 copy.15
  2.1 0.7 reshape.7.cells
  2.8 154.7 %shard_map.122 = (f32[32,4,512]{2,1,0:T(4,128)}, f32[3,32,512]{2,1,0:T(8,128)}) custom-call(f32[32,4,512]{2,1,0:T(4,128)} %part.1, f32[3,32,512]{2,1,0:T(8,128)} %bitcast.9, f32[32,128]{1,0:T(8,128)} %reshape.7.cells, f32[16,128]{1,0:T(8,128)} %pad.9.top, s32[4]{0:T(128)} %act_ids.1, s32[1]{0:T(128)S(6)} %copy.18.act_cnt, s32[4,64]{1,0:T(4,128)} %cell_lists.1, ...), custom_call_target="tpu_custom_call" | custom-call | tf_op jit(solution)/shard_map/pallas_call | solution.py:556
  157.4 0.0 copy-start
  157.5 1.7 %copy.19 = f32[32,4,512]{2,1,0:T(4,128)} copy(f32[32,4,512]{2,1,0:T(4,128)} %get-tuple-element.8) | data formatting | bytes 524288
  159.2 0.0 copy-done
  159.2 0.7 copy.20
  (1 shorter events, 0.0 us)
Async XLA Ops:
  0.6 0.7 copy-start.2
  0.6 1.3 copy-start.1
  157.4 1.7 %copy-start = (f32[3,32,512]{2,1,0:T(8,128)S(1)}, f32[3,32,512]{2,1,0:T(8,128)}, u32[]{:S(2)}) copy-start(f32[3,32,512]{2,1,0:T(8,128)} %get-tuple-element.5) | copy-start | bytes 589828

commit v2 on v1

--- a/solution.py
+++ b/solution.py
@@ -61,7 +61,7 @@
     part, vel, cells, top, act_ids, act_cnt, cell_lists, cell_req, leaf_req, leaf_lists, targets,
     outp, outv,
     p_all, v_all, v_y, c_all, t_all, top_m, codes_v, codes_s, l_send,
-    l0, l1, l2, l3, k0, k1, k2, k3, p_rec, pts, acc, own, chosen, picks, near,
+    l0, l1, l2, l3, k0, k1, k2, k3, p_rec, pts, acc, own, near,
     p_ss, p_rs, c_ss, c_rs, v_ss, v_rs, t_ss, t_rs, d_ss, d_rs, vy_ss, vy_rs,
     cy_ss, cy_rs, l_ss, l_rs, pr_ss, pr_rs, kz_ss, kz_rs, ky_ss, ky_rs, loc,
 ):
@@ -79,13 +79,15 @@
         return ((y + d) % NY) * NZ + z
 
     own_p = pltpu.make_async_copy(part, p_all.at[z], loc.at[0])
-    own_v = pltpu.make_async_copy(vel, v_y.at[y], loc.at[1])
-    own_c = pltpu.make_async_copy(cells, c_all.at[bulk], loc.at[2])
-    own_t = pltpu.make_async_copy(top, t_all.at[leaf], loc.at[3])
+    own_v = pltpu.make_async_copy(vel, v_y.at[pl.ds(y * 3, 3)], loc.at[1])
     own_p.start()
     own_v.start()
-    own_c.start()
-    own_t.start()
+    c_all[bulk, pl.ds(0, 8), :] = cells[pl.ds(0, 8), :]
+    c_all[bulk, pl.ds(8, 8), :] = jnp.concatenate(
+        [cells[pl.ds(8, 2), :], jnp.zeros((6, 256), jnp.float32)], axis=0
+    )
+    t_all[leaf] = jnp.zeros((16, 128), jnp.float32)
+    t_all[leaf, pl.ds(0, 10), pl.ds(0, 64)] = top[...]
 
     def code_of(a, e):
         f = leaf_lists[a, e]
@@ -106,13 +108,13 @@
     def greet(dev):
         pl.semaphore_signal(barrier, inc=1, device_id=dev, device_id_type=MESH)
 
-    for d in range(1, NZ):
+    for d in (1, 2, NZ - 2, NZ - 1):
         greet({"bulk": row_peer(d)})
     for d in range(1, NY):
         greet({"bulk": col_peer(d)})
     for d in range(1, NL):
         greet({"leaf": (leaf + d) % NL})
-    pl.semaphore_wait(barrier, NZ + NY + NL - 3)
+    pl.semaphore_wait(barrier, 4 + NY + NL - 2)
 
     def remote(src, dst, ss, rs, dev):
         return pltpu.make_async_remote_copy(
@@ -134,27 +136,35 @@
 
     def c_copy(way, h):
         at = c_all.at[y * NZ + ring_src(way, h)]
-        src = cells if isinstance(h, int) and h == 0 else at
-        return remote(src, at, c_ss.at[way, h], c_rs.at[way, h], ring_dev(way))
+        return remote(at, at, c_ss.at[way, h], c_rs.at[way, h], ring_dev(way))
 
     def v_copy(way, h, sub):
         at = v_all.at[ring_src(way, h), sub]
         return remote(at, at, v_ss.at[way, h, sub], v_rs.at[way, h, sub], ring_dev(way))
 
     def t_copy(d):
-        return remote(top, t_all.at[leaf], t_ss.at[d], t_rs.at[d], {"leaf": (leaf + d) % NL})
+        return remote(t_all.at[leaf], t_all.at[leaf], t_ss.at[d], t_rs.at[d], {"leaf": (leaf + d) % NL})
 
     def d_copy(d):
         return remote(
             codes_v.at[y], codes_v.at[y], d_ss.at[d], d_rs.at[d], {"bulk": col_peer(d)}
         )
 
-    def vy_copy(d):
-        return remote(vel, v_y.at[y], vy_ss.at[d], vy_rs.at[d], {"bulk": col_peer(d)})
-
-    def cy_copy(d):
-        blk = c_all.at[pl.ds(y * NZ, NZ)]
-        return remote(blk, blk, cy_ss.at[d], cy_rs.at[d], {"bulk": col_peer(d)})
+    def y_gather(ref, size, ss, rs, k):
+        half = (size + 1) // 2
+        if k < 2:
+            cut = ref.at[pl.ds(y * size, size)]
+        elif k == 2:
+            cut = ref.at[pl.ds(((y + NY - 1) % NY) * size, half)]
+        else:
+            cut = ref.at[pl.ds(((y + 1) % NY) * size + half, size - half)]
+        return remote(cut, cut, ss, rs, {"bulk": col_peer(1 if k % 2 == 0 else NY - 1)})
+
+    def vy_copy(k):
+        return y_gather(v_y, 3, vy_ss.at[k], vy_rs.at[k], k)
+
+    def cy_copy(k):
+        return y_gather(c_all, NZ, cy_ss.at[k], cy_rs.at[k], k)
 
     def l_copy(a, d):
         return remote(
@@ -162,18 +172,51 @@
             {"bulk": col_peer(d)},
         )
 
-    def pr_copy(d):
-        return remote(
-            p_rec.at[y], p_rec.at[y], pr_ss.at[d], pr_rs.at[d], {"bulk": col_peer(d)}
-        )
-
-    def kz_copy(a, d):
-        at = k_all[a].at[y, z]
-        return remote(at, at, kz_ss.at[a, d], kz_rs.at[a, d], {"bulk": row_peer(d)})
-
-    def ky_copy(a, d):
-        at = k_all[a].at[y]
-        return remote(at, at, ky_ss.at[a, d], ky_rs.at[a, d], {"bulk": col_peer(d)})
+    def pr_copy(k):
+        return y_gather(p_rec, NB, pr_ss.at[k], pr_rs.at[k], k)
+
+    def ky_copy(a, k):
+        return y_gather(k_all[a], NZ, ky_ss.at[a, k], ky_rs.at[a, k], k)
+
+    def kz_copy(a, dist):
+        if dist <= NZ // 2:
+            hop = 1 if dist == 1 else 2
+            at, to = (z + NZ - (dist - hop)) % NZ, hop
+        else:
+            back = NZ - dist
+            hop = 1 if back == 1 else 2
+            at, to = (z + (back - hop)) % NZ, NZ - hop
+        cut = k_all[a].at[y * NZ + at]
+        return remote(cut, cut, kz_ss.at[a, dist], kz_rs.at[a, dist], {"bulk": row_peer(to)})
+
+    def k_start(a):
+        for dist in (1, NZ - 1, 2, NZ - 2):
+            kz_copy(a, dist).start()
+
+    def k_step(a, step):
+        for dist in (2 * step - 1, NZ - 2 * step + 1, 2 * step, NZ - 2 * step):
+            kz_copy(a, dist).wait_recv()
+        sends = [2 * step + 1, NZ - 2 * step - 1, 2 * step + 2]
+        if step < NZ // 4 - 1:
+            sends.append(NZ - 2 * step - 2)
+        for dist in sends:
+            kz_copy(a, dist).start()
+
+    def y_send(a):
+        for dist in (NZ // 2 - 1, NZ // 2, NZ // 2 + 1):
+            kz_copy(a, dist).wait_recv()
+        for k in range(2):
+            ky_copy(a, k).start()
+
+    def y_forward(copy):
+        for k in range(2):
+            copy(k).wait_recv()
+        for k in range(2, 4):
+            copy(k).start()
+
+    def y_done(copy):
+        for k in range(2, 4):
+            copy(k).wait_recv()
 
     for d in range(1, NL):
         t_copy(d).start()
@@ -184,8 +227,9 @@
     for sub in range(SUBS):
         for way in range(2):
             p_copy(way, 0, sub, True).start()
-    for d in range(1, NY):
-        vy_copy(d).start()
+    own_v.wait()
+    for k in range(2):
+        vy_copy(k).start()
 
     for a in range(ACT):
         bucket = part[act_ids[a]]
@@ -198,7 +242,6 @@
 
         lax.fori_loop(0, 3, spread, 0)
 
-    own_t.wait()
     for d in range(1, NL):
         t_copy(d).wait_recv()
     half = lax.broadcasted_iota(jnp.int32, (16, 128), 1) < 64
@@ -230,7 +273,7 @@
                 acc[a, c, at, :] = accs[c]
             return 0
 
-        lax.fori_loop(0, count, step, 0)
+        lax.fori_loop(0, count, step, 0, unroll=2)
 
     def near_part(a, o0, count):
         cut = pl.ds(pl.multiple_of((a // 2) * 128, 128), 128)
@@ -248,7 +291,7 @@
                 acc[a, c, at, :] = accs[c]
             return 0
 
-        lax.fori_loop(0, count, step, 0)
+        lax.fori_loop(0, count, step, 0, unroll=4)
 
     def p_event(i):
         h = i // SUBS
@@ -282,8 +325,6 @@
                 def _():
                     c_copy(way, i + 1).start()
 
-    own_c.wait()
-
     def first_events(i, _):
         c_event(i)
         p_event(i)
@@ -291,8 +332,9 @@
         return 0
 
     lax.fori_loop(0, 8, first_events, 0)
-    for d in range(1, NY):
-        cy_copy(d).start()
+    y_forward(vy_copy)
+    for k in range(2):
+        cy_copy(k).start()
 
     def more_events(i, _):
         p_event(i)
@@ -301,43 +343,40 @@
 
     lax.fori_loop(8, 16, more_events, 0)
 
-    own_v.wait()
-    for d in range(1, NY):
-        vy_copy(d).wait_recv()
+    y_done(vy_copy)
+    y_forward(cy_copy)
 
     def pick_row(j, _):
         shift = (targets[j] - bulk) & 63
         to_z = (z + shift) & 15
         from_y = ((y * NZ + to_z - shift) & 63) >> 4
         for c in range(3):
-            v_all[z, c, pl.ds(j, 1), :] = v_y[from_y, c, pl.ds(j, 1), :]
-        return 0
-
-    lax.fori_loop(0, NB, pick_row, 0)
+            v_all[z, c, pl.ds(j, 1), :] = v_y[from_y * 3 + c, pl.ds(j, 1), :]
+        return 0
+
+    lax.fori_loop(0, NB, pick_row, 0, unroll=8)
     lax.fori_loop(16, 24, more_events, 0)
 
-    for d in range(1, NY):
-        cy_copy(d).wait_recv()
-
-    def pick_cell(i, _):
-        f = cell_lists[i // CPER, i % CPER]
-        peer = f >> 4
-        col = cell_req[f & 15, peer] & 255
-        chosen[pl.ds(i, 1), :] = c_all[peer, pl.ds(col >> 3, 1), :]
-        picks[pl.ds(i, 1), :] = jnp.full((1, 128), col & 7, jnp.int32)
-        return 0
-
-    lax.fori_loop(0, ACT * CPER, pick_cell, 0)
-    got = chosen[...]
-    group = picks[...]
-    packed = jnp.where(group == 0, got, 0.0)
-    for g in range(1, 8):
-        packed = jnp.where(group == g, pltpu.roll(got, 128 - 16 * g, 1), packed)
-    near[...] = jnp.transpose(packed)
+    y_done(cy_copy)
+    lane16 = lax.broadcasted_iota(jnp.int32, (16, 128), 1)
+    lane256 = lax.broadcasted_iota(jnp.int32, (16, 256), 1)
+    for part_at in range(2):
+
+        def pick_cell(i, got, part_at=part_at):
+            f = cell_lists[part_at * 2 + i // CPER, i % CPER]
+            peer = f >> 4
+            col = cell_req[f & 15, peer] & 255
+            one = jnp.where(lane256 == col, c_all[peer], 0.0)
+            return jnp.where(lane16 == i, jnp.sum(one, axis=1, keepdims=True), got)
+
+        near[:, pl.ds(part_at * 128, 128)] = lax.fori_loop(
+            0, 128, pick_cell, jnp.zeros((16, 128), jnp.float32), unroll=8
+        )
 
     def last_events(i, _):
         p_event(i)
         self_top(i // 8, (i % 8) * 8, 8)
+        near_part((i - 24) // 2, (i % 2) * (OCT // 2), OCT // 2)
         return 0
 
     lax.fori_loop(24, 32, last_events, 0)
@@ -345,7 +384,7 @@
     own_p.wait()
     for d in range(1, NY):
         d_copy(d).wait_recv()
-    codes_copy = pltpu.make_async_copy(codes_v, codes_s, loc.at[4])
+    codes_copy = pltpu.make_async_copy(codes_v, codes_s, loc.at[2])
     codes_copy.start()
     codes_copy.wait()
 
@@ -360,14 +399,14 @@
                 l_send[d - 1, a, e] = leaf_at(codes_s[to_y, a, e])
                 return 0
 
-            lax.fori_loop(0, LPER, fill, 0)
+            lax.fori_loop(0, LPER, fill, 0, unroll=True)
             l_copy(a, d).start()
 
         def fill_own(e, _, a=a):
             l_rec[a][y, e] = leaf_at(code_of(a, e))
             return 0
 
-        lax.fori_loop(0, LPER, fill_own, 0)
+        lax.fori_loop(0, LPER, fill_own, 0, unroll=True)
 
     for way in range(2):
         for sub in range(3):
@@ -375,15 +414,12 @@
 
     def pick_moved(j, _):
         from_z = (bulk - (targets[j] - bulk)) & 15
-        p_rec[y, j] = p_all[from_z, j]
-        return 0
-
-    lax.fori_loop(0, NB, pick_moved, 0)
-    for d in range(1, NY):
-        pr_copy(d).start()
-
-    for a in range(ACT):
-        near_part(a, 0, OCT)
+        p_rec[y * NB + j] = p_all[from_z, j]
+        return 0
+
+    lax.fori_loop(0, NB, pick_moved, 0, unroll=8)
+    for k in range(2):
+        pr_copy(k).start()
 
     def v_event(i):
         h = i // 3
@@ -399,18 +435,13 @@
             def _():
                 v_copy(way, h + 1, sub).start()
 
-    def y_send(a):
-        def wait_one(d, _):
-            kz_copy(a, d).wait_recv()
-            return 0
-
-        lax.fori_loop(1, NZ, wait_one, 0)
-        for d in range(1, NY):
-            ky_copy(a, d).start()
-
     for a in range(ACT):
         for d in range(1, NY):
             l_copy(a, d).wait_recv()
+        if a >= 2:
+            y_send(a - 2)
+        if a == 3:
+            y_forward(pr_copy)
 
         def block(e, _, a=a):
             from_y = (code_of(a, e) >> 9) & 3
@@ -425,11 +456,24 @@
                     acc[a, c, at, :] = accs[c]
                 return 0
 
-            lax.fori_loop(0, OCT, step, 0)
-
-            @pl.when(e % 2 == 1)
+            lax.fori_loop(0, OCT, step, 0, unroll=4)
+
+            @pl.when(e % 2 == 0)
             def _():
                 v_event(a * 3 + e // 2)
+
+            if a >= 1:
+                for step_at in (1, 2, 3):
+
+                    @pl.when(e == 2 * step_at - 1)
+                    def _(step_at=step_at):
+                        k_step(a - 1, step_at)
+
+            if a >= 2:
+
+                @pl.when(e == 4)
+                def _():
+                    y_forward(functools.partial(ky_copy, a - 2))
 
             return 0
 
@@ -438,49 +482,55 @@
         ident = jnp.where(a < act_cnt[0], act_ids[a], -1).astype(jnp.float32)
         for c in range(3):
             pull = jnp.sum(jnp.transpose(acc[a, c]), axis=0, keepdims=True)
-            k_all[a][y, z, pl.ds(c, 1), :] = step_time * pull * alive
-        k_all[a][y, z, pl.ds(3, 1), :] = jnp.full((1, 512), ident, jnp.float32)
-
-        def send_one(d, _, a=a):
-            kz_copy(a, d).start()
-            return 0
-
-        lax.fori_loop(1, NZ, send_one, 0)
-        if a > 0:
-            y_send(a - 1)
+            k_all[a][bulk, pl.ds(c, 1), :] = step_time * pull * alive
+        k_all[a][bulk, pl.ds(3, 1), :] = jnp.full((1, 512), ident, jnp.float32)
+
+        k_start(a)
+
+    last = ACT - 1
+    y_send(last - 1)
+    v_event(12)
+    k_step(last, 1)
+    v_event(13)
+    k_step(last, 2)
+    y_forward(functools.partial(ky_copy, last - 1))
+    v_event(14)
+    k_step(last, 3)
+    v_event(15)
+    y_send(last)
+    v_event(16)
+    v_event(17)
+    y_forward(functools.partial(ky_copy, last))
 
     def tail_events(i, _):
         v_event(i)
         return 0
 
-    lax.fori_loop(12, 24, tail_events, 0)
-    y_send(ACT - 1)
-    for d in range(1, NY):
-        pr_copy(d).wait_recv()
+    lax.fori_loop(18, 24, tail_events, 0)
+    y_done(pr_copy)
     for a in range(ACT):
-        for d in range(1, NY):
-            ky_copy(a, d).wait_recv()
+        y_done(functools.partial(ky_copy, a))
 
     def place(j, _):
         source = (bulk - (targets[j] - bulk)) & 63
         from_y = source >> 4
         from_z = source & 15
         number = j.astype(jnp.float32)
-        hits = [k_all[a][from_y, from_z, pl.ds(3, 1), :] == number for a in range(ACT)]
+        hits = [k_all[a][source, pl.ds(3, 1), :] == number for a in range(ACT)]
         for c in range(3):
             speed = v_all[from_z, c, pl.ds(j, 1), :]
             kick = jnp.zeros((1, 512), jnp.float32)
             for a in range(ACT):
                 kick = kick + jnp.where(
-                    hits[a], k_all[a][from_y, from_z, pl.ds(c, 1), :], 0.0
+                    hits[a], k_all[a][source, pl.ds(c, 1), :], 0.0
                 )
             speed = speed + kick
             outv[c, pl.ds(j, 1), :] = speed
-            outp[j, pl.ds(c, 1), :] = p_rec[from_y, j, pl.ds(c, 1), :] + step_time * speed
-        outp[j, pl.ds(3, 1), :] = p_rec[from_y, j, pl.ds(3, 1), :]
-        return 0
-
-    lax.fori_loop(0, NB, place, 0)
+            outp[j, pl.ds(c, 1), :] = p_rec[from_y * NB + j, pl.ds(c, 1), :] + step_time * speed
+        outp[j, pl.ds(3, 1), :] = p_rec[from_y * NB + j, pl.ds(3, 1), :]
+        return 0
+
+    lax.fori_loop(0, NB, place, 0, unroll=4)
 
     for d in range(1, NL):
         t_copy(d).wait_send()
@@ -518,19 +568,17 @@
             c_copy(1, h).wait_send()
     for d in range(1, NY):
         d_copy(d).wait_send()
-        vy_copy(d).wait_send()
-        cy_copy(d).wait_send()
-        pr_copy(d).wait_send()
         for a in range(ACT):
             l_copy(a, d).wait_send()
-            ky_copy(a, d).wait_send()
+    for k in range(4):
+        vy_copy(k).wait_send()
+        cy_copy(k).wait_send()
+        pr_copy(k).wait_send()
+        for a in range(ACT):
+            ky_copy(a, k).wait_send()
     for a in range(ACT):
-
-        def kz_sent(d, _, a=a):
-            kz_copy(a, d).wait_send()
-            return 0
-
-        lax.fori_loop(1, NZ, kz_sent, 0)
+        for dist in range(1, NZ):
+            kz_copy(a, dist).wait_send()
 
 
 def on_device(
@@ -547,8 +595,6 @@
     targets,
 ):
     speeds = jnp.transpose(velocities, (1, 0, 2))
-    cells = jnp.pad(cell_table.T, ((0, 0), (0, 6))).reshape(32, 128)
-    top = jnp.pad(top_cells, ((0, 6), (0, 64)))
     vmem = pl.BlockSpec(memory_space=pltpu.VMEM)
     smem = pl.BlockSpec(memory_space=pltpu.SMEM)
     f32 = jnp.float32
@@ -564,8 +610,8 @@
         scratch_shapes=[
             pltpu.VMEM((NZ, NB, 4, 512), f32),
             pltpu.VMEM((NZ, 3, NB, 512), f32),
-            pltpu.VMEM((NY, 3, NB, 512), f32),
-            pltpu.VMEM((NY * NZ, 32, 128), f32),
+            pltpu.VMEM((NY * 3, NB, 512), f32),
+            pltpu.VMEM((NY * NZ, 16, 256), f32),
             pltpu.VMEM((NL, 16, 128), f32),
             pltpu.VMEM((16, 512), f32),
             pltpu.VMEM((NY, 8, 128), jnp.int32),
@@ -573,15 +619,13 @@
             pltpu.VMEM((NY - 1, ACT, LPER, 4, 512), f32),
         ]
         + [pltpu.VMEM((NY, LPER, 4, 512), f32)] * ACT
-        + [pltpu.VMEM((NY, NZ, 4, 512), f32)] * ACT
+        + [pltpu.VMEM((NY * NZ, 4, 512), f32)] * ACT
         + [
-            pltpu.VMEM((NY, NB, 4, 512), f32),
+            pltpu.VMEM((NY * NB, 4, 512), f32),
             pltpu.VMEM((ACT, 3, 512, 128), f32),
             pltpu.VMEM((ACT, 3, 512, 128), f32),
             pltpu.VMEM((ACT, 8, 512), f32),
-            pltpu.VMEM((ACT * CPER, 128), f32),
-            pltpu.VMEM((ACT * CPER, 128), jnp.int32),
-            pltpu.VMEM((128, ACT * CPER), f32),
+            pltpu.VMEM((16, ACT * CPER), f32),
             dma((2, 8, SUBS)),
             dma((2, 8, SUBS)),
             dma((2, 8)),
@@ -612,8 +656,8 @@
     )(
         particles,
         speeds,
-        cells,
-        top,
+        cell_table,
+        top_cells,
         active_ids,
         active_count,
         cell_lists,

time: 160 us -> 159 us (level)
  no operation moved by 1% of the time
where the time goes in v2:
time: 159 us; the launch traced here: 158 us
  Pallas kernels  155 us (97%)
  local copies, waits for them, and re-layouts  2.39 us (2%)
    pallas_call x1, Pallas kernels, on_device(): pl.pallas_call(kernel, out_shape=(jax.ShapeDtypeStruct((NB, 4, 512), f32)...  155 us

profile of v2, /device:TPU:6, one launch (start us, length us, event | category | flops | bytes accessed | tf_op | source)
XLA Modules:
  0.0 158.4 jit_solution(13375262776707426475)
XLA Ops:
  1.3 154.7 %shard_map.122 = (f32[32,4,512]{2,1,0:T(4,128)}, f32[3,32,512]{2,1,0:T(8,128)}) custom-call(f32[32,4,512]{2,1,0:T(4,128)} %part.1, f32[3,32,512]{2,1,0:T(8,128)} %bitcast.8, f32[10,256]{1,0:T(8,128)} %cells.1, f32[10,64]{1,0:T(8,128)} %top.1, s32[4]{0:T(128)} %act_ids.1, s32[1]{0:T(128)S(6)} %copy.15.act_cnt, s32[4,64]{1,0:T(4,128)} %cell_lists.1, ...), custom_call_target="tpu_custom_call" | custom-call | tf_op jit(solution)/shard_map/pallas_call | solution.py:602
  156.0 0.0 copy-start
  156.0 1.7 %copy.16 = f32[32,4,512]{2,1,0:T(4,128)} copy(f32[32,4,512]{2,1,0:T(4,128)} %get-tuple-element.8) | data formatting | bytes 524288
  157.7 0.0 copy-done
  157.7 0.7 copy.17
Async XLA Ops:
  156.0 1.7 %copy-start = (f32[3,32,512]{2,1,0:T(8,128)S(1)}, f32[3,32,512]{2,1,0:T(8,128)}, u32[]{:S(2)}) copy-start(f32[3,32,512]{2,1,0:T(8,128)} %get-tuple-element.5) | copy-start | bytes 589828

commit v3 on v2

--- a/solution.py
+++ b/solution.py
@@ -78,13 +78,19 @@
     def col_peer(d):
         return ((y + d) % NY) * NZ + z
 
+    def ident_of(a):
+        return jnp.where(a < act_cnt[0], act_ids[a], -1).astype(jnp.float32)
+
     own_p = pltpu.make_async_copy(part, p_all.at[z], loc.at[0])
     own_v = pltpu.make_async_copy(vel, v_y.at[pl.ds(y * 3, 3)], loc.at[1])
     own_p.start()
     own_v.start()
     c_all[bulk, pl.ds(0, 8), :] = cells[pl.ds(0, 8), :]
     c_all[bulk, pl.ds(8, 8), :] = jnp.concatenate(
-        [cells[pl.ds(8, 2), :], jnp.zeros((6, 256), jnp.float32)], axis=0
+        [cells[pl.ds(8, 2), :]]
+        + [jnp.full((1, 256), ident_of(a), jnp.float32) for a in range(ACT)]
+        + [jnp.zeros((2, 256), jnp.float32)],
+        axis=0,
     )
     t_all[leaf] = jnp.zeros((16, 128), jnp.float32)
     t_all[leaf, pl.ds(0, 10), pl.ds(0, 64)] = top[...]
@@ -108,13 +114,13 @@
     def greet(dev):
         pl.semaphore_signal(barrier, inc=1, device_id=dev, device_id_type=MESH)
 
-    for d in (1, 2, NZ - 2, NZ - 1):
+    for d in (1, 2, 4, 8, NZ - 4, NZ - 2, NZ - 1):
         greet({"bulk": row_peer(d)})
     for d in range(1, NY):
         greet({"bulk": col_peer(d)})
     for d in range(1, NL):
         greet({"leaf": (leaf + d) % NL})
-    pl.semaphore_wait(barrier, 4 + NY + NL - 2)
+    pl.semaphore_wait(barrier, 7 + NY + NL - 2)
 
     def remote(src, dst, ss, rs, dev):
         return pltpu.make_async_remote_copy(
@@ -175,38 +181,36 @@
     def pr_copy(k):
         return y_gather(p_rec, NB, pr_ss.at[k], pr_rs.at[k], k)
 
-    def ky_copy(a, k):
-        return y_gather(k_all[a], NZ, ky_ss.at[a, k], ky_rs.at[a, k], k)
-
-    def kz_copy(a, dist):
-        if dist <= NZ // 2:
-            hop = 1 if dist == 1 else 2
-            at, to = (z + NZ - (dist - hop)) % NZ, hop
-        else:
-            back = NZ - dist
-            hop = 1 if back == 1 else 2
-            at, to = (z + (back - hop)) % NZ, NZ - hop
-        cut = k_all[a].at[y * NZ + at]
-        return remote(cut, cut, kz_ss.at[a, dist], kz_rs.at[a, dist], {"bulk": row_peer(to)})
-
-    def k_start(a):
-        for dist in (1, NZ - 1, 2, NZ - 2):
-            kz_copy(a, dist).start()
-
-    def k_step(a, step):
-        for dist in (2 * step - 1, NZ - 2 * step + 1, 2 * step, NZ - 2 * step):
-            kz_copy(a, dist).wait_recv()
-        sends = [2 * step + 1, NZ - 2 * step - 1, 2 * step + 2]
-        if step < NZ // 4 - 1:
-            sends.append(NZ - 2 * step - 2)
-        for dist in sends:
-            kz_copy(a, dist).start()
+    def ky_copy(a, d):
+        cut = k_all[a].at[pl.ds(y * NZ, NZ)]
+        return remote(cut, cut, ky_ss.at[a, d], ky_rs.at[a, d], {"bulk": col_peer(d)})
+
+    far = (4, 8, 12)
+    close = (1, NZ - 1, 2)
+
+    def kz_copy(a, hop, base=0):
+        cut = k_all[a].at[y * NZ + (z + NZ - base) % NZ]
+        dist = (base + hop) % NZ
+        return remote(cut, cut, kz_ss.at[a, dist], kz_rs.at[a, dist], {"bulk": row_peer(hop)})
+
+    def k_far(a):
+        for hop in (8, 4, 12):
+            kz_copy(a, hop).start()
+        for hop in close:
+            kz_copy(a, hop).start()
+
+    def k_close(a):
+        for base in far:
+            kz_copy(a, base).wait_recv()
+            for hop in close:
+                kz_copy(a, hop, base).start()
 
     def y_send(a):
-        for dist in (NZ // 2 - 1, NZ // 2, NZ // 2 + 1):
-            kz_copy(a, dist).wait_recv()
-        for k in range(2):
-            ky_copy(a, k).start()
+        for base in (0,) + far:
+            for hop in close:
+                kz_copy(a, hop, base).wait_recv()
+        for d in (2, 1, 3):
+            ky_copy(a, d).start()
 
     def y_forward(copy):
         for k in range(2):
@@ -438,8 +442,6 @@
     for a in range(ACT):
         for d in range(1, NY):
             l_copy(a, d).wait_recv()
-        if a >= 2:
-            y_send(a - 2)
         if a == 3:
             y_forward(pr_copy)
 
@@ -456,75 +458,130 @@
                     acc[a, c, at, :] = accs[c]
                 return 0
 
-            lax.fori_loop(0, OCT, step, 0, unroll=4)
-
-            @pl.when(e % 2 == 0)
+            lax.fori_loop(0, OCT, step, 0, unroll=8)
+
+            first = a * 4 - (a > 0)
+
+            @pl.when(e % 2 == 1)
             def _():
-                v_event(a * 3 + e // 2)
-
-            if a >= 1:
-                for step_at in (1, 2, 3):
-
-                    @pl.when(e == 2 * step_at - 1)
-                    def _(step_at=step_at):
-                        k_step(a - 1, step_at)
+                v_event(first + (a > 0) + e // 2)
+
+            if a > 0:
+
+                @pl.when(e == 0)
+                def _():
+                    v_event(first)
 
             if a >= 2:
 
-                @pl.when(e == 4)
+                @pl.when(e == 3)
                 def _():
-                    y_forward(functools.partial(ky_copy, a - 2))
+                    k_close(a - 2)
+
+            if a == 3:
+
+                @pl.when(e == 2)
+                def _():
+                    y_send(0)
 
             return 0
 
         lax.fori_loop(0, LPER, block, 0)
-        alive = jnp.where(a < act_cnt[0], 1.0, 0.0)
-        ident = jnp.where(a < act_cnt[0], act_ids[a], -1).astype(jnp.float32)
+        alive = jnp.where(a < act_cnt[0], step_time, 0.0)
         for c in range(3):
-            pull = jnp.sum(jnp.transpose(acc[a, c]), axis=0, keepdims=True)
-            k_all[a][bulk, pl.ds(c, 1), :] = step_time * pull * alive
-        k_all[a][bulk, pl.ds(3, 1), :] = jnp.full((1, 512), ident, jnp.float32)
-
-        k_start(a)
-
-    last = ACT - 1
-    y_send(last - 1)
-    v_event(12)
-    k_step(last, 1)
-    v_event(13)
-    k_step(last, 2)
-    y_forward(functools.partial(ky_copy, last - 1))
-    v_event(14)
-    k_step(last, 3)
-    v_event(15)
-    y_send(last)
-    v_event(16)
-    v_event(17)
-    y_forward(functools.partial(ky_copy, last))
-
-    def tail_events(i, _):
-        v_event(i)
+            pull = jnp.sum(jnp.transpose(acc[a, c]), axis=0, keepdims=True) * alive
+            for b in range(4):
+                row, col = divmod(c * 4 + b, 3)
+                k_all[a][bulk, pl.ds(row, 1), pl.ds(col * 128, 128)] = pull[
+                    :, b * 128 : (b + 1) * 128
+                ]
+        k_far(a)
+
+    def v_events(lo, hi):
+        def go(i, _):
+            v_event(i)
+            return 0
+
+        lax.fori_loop(lo, hi, go, 0)
+
+    for d in range(1, NL):
+        t_copy(d).wait_send()
+
+    def p_sent(i, _):
+        h = i // SUBS
+        sub = i % SUBS
+        for way in range(2):
+            mine = (sub < SUBS // 2) if way == 0 else (sub >= SUBS // 2)
+
+            @pl.when((h < NZ // 2 - 1) | mine)
+            def _():
+                p_copy(way, h, sub).wait_send()
+
         return 0
 
-    lax.fori_loop(18, 24, tail_events, 0)
+    lax.fori_loop(0, 32, p_sent, 0)
+    v_events(15, 16)
+    y_send(1)
+    v_events(16, 17)
+    k_close(2)
+    v_events(17, 18)
+    for h in range(NZ // 2):
+        c_copy(0, h).wait_send()
+        if h < NZ // 2 - 1:
+            c_copy(1, h).wait_send()
+    for k in range(4):
+        vy_copy(k).wait_send()
+        cy_copy(k).wait_send()
+    for d in range(1, NY):
+        d_copy(d).wait_send()
+        for a in range(ACT):
+            l_copy(a, d).wait_send()
+    v_events(18, 19)
+    y_send(2)
+    k_close(3)
+    v_events(19, 21)
     y_done(pr_copy)
+    for k in range(4):
+        pr_copy(k).wait_send()
+    y_send(3)
+    v_events(21, 24)
+
+    def v_sent(i, _):
+        h = i // 3
+        sub = i % 3
+        for way in range(2):
+            mine = (sub == 0) if way == 0 else (sub > 0)
+
+            @pl.when((h < NZ // 2 - 1) | mine)
+            def _():
+                v_copy(way, h, sub).wait_send()
+
+        return 0
+
+    lax.fori_loop(0, 24, v_sent, 0)
     for a in range(ACT):
-        y_done(functools.partial(ky_copy, a))
+        for dist in range(1, NZ):
+            kz_copy(a, dist).wait_send()
+    for a in range(ACT):
+        for d in range(1, NY):
+            ky_copy(a, d).wait_recv()
 
     def place(j, _):
         source = (bulk - (targets[j] - bulk)) & 63
         from_y = source >> 4
         from_z = source & 15
         number = j.astype(jnp.float32)
-        hits = [k_all[a][source, pl.ds(3, 1), :] == number for a in range(ACT)]
+        hits = [c_all[source, pl.ds(10 + a, 1), pl.ds(0, 128)] == number for a in range(ACT)]
         for c in range(3):
-            speed = v_all[from_z, c, pl.ds(j, 1), :]
-            kick = jnp.zeros((1, 512), jnp.float32)
-            for a in range(ACT):
-                kick = kick + jnp.where(
-                    hits[a], k_all[a][source, pl.ds(c, 1), :], 0.0
-                )
-            speed = speed + kick
+            parts = []
+            for b in range(4):
+                row, col = divmod(c * 4 + b, 3)
+                kick = jnp.zeros((1, 128), jnp.float32)
+                for a in range(ACT):
+                    got = k_all[a][source, pl.ds(row, 1), pl.ds(col * 128, 128)]
+                    kick = kick + jnp.where(hits[a], got, 0.0)
+                parts.append(kick)
+            speed = v_all[from_z, c, pl.ds(j, 1), :] + jnp.concatenate(parts, axis=1)
             outv[c, pl.ds(j, 1), :] = speed
             outp[j, pl.ds(c, 1), :] = p_rec[from_y * NB + j, pl.ds(c, 1), :] + step_time * speed
         outp[j, pl.ds(3, 1), :] = p_rec[from_y * NB + j, pl.ds(3, 1), :]
@@ -532,53 +589,9 @@
 
     lax.fori_loop(0, NB, place, 0, unroll=4)
 
-    for d in range(1, NL):
-        t_copy(d).wait_send()
-
-    def p_sent(i, _):
-        h = i // SUBS
-        sub = i % SUBS
-        for way in range(2):
-            mine = (sub < SUBS // 2) if way == 0 else (sub >= SUBS // 2)
-
-            @pl.when((h < NZ // 2 - 1) | mine)
-            def _():
-                p_copy(way, h, sub).wait_send()
-
-        return 0
-
-    lax.fori_loop(0, 32, p_sent, 0)
-
-    def v_sent(i, _):
-        h = i // 3
-        sub = i % 3
-        for way in range(2):
-            mine = (sub == 0) if way == 0 else (sub > 0)
-
-            @pl.when((h < NZ // 2 - 1) | mine)
-            def _():
-                v_copy(way, h, sub).wait_send()
-
-        return 0
-
-    lax.fori_loop(0, 24, v_sent, 0)
-    for h in range(NZ // 2):
-        c_copy(0, h).wait_send()
-        if h < NZ // 2 - 1:
-            c_copy(1, h).wait_send()
-    for d in range(1, NY):
-        d_copy(d).wait_send()
-        for a in range(ACT):
-            l_copy(a, d).wait_send()
-    for k in range(4):
-        vy_copy(k).wait_send()
-        cy_copy(k).wait_send()
-        pr_copy(k).wait_send()
-        for a in range(ACT):
-            ky_copy(a, k).wait_send()
     for a in range(ACT):
-        for dist in range(1, NZ):
-            kz_copy(a, dist).wait_send()
+        for d in range(1, NY):
+            ky_copy(a, d).wait_send()
 
 
 def on_device(
@@ -619,7 +632,7 @@
             pltpu.VMEM((NY - 1, ACT, LPER, 4, 512), f32),
         ]
         + [pltpu.VMEM((NY, LPER, 4, 512), f32)] * ACT
-        + [pltpu.VMEM((NY * NZ, 4, 512), f32)] * ACT
+        + [pltpu.VMEM((NY * NZ, 4, 384), f32)] * ACT
         + [
             pltpu.VMEM((NY * NB, 4, 512), f32),
             pltpu.VMEM((ACT, 3, 512, 128), f32),

time: 159 us -> 135 us (0.85)
  Pallas kernels: 155 us -> 131 us
    pallas_call x1, Pallas kernels: 155 us -> 131 us  [on_device(): pl.pallas_call(kernel, out_shape=(jax.ShapeDtypeStruct((NB, 4, 512), f32)...]
where the time goes in v3:
time: 135 us
  Pallas kernels  131 us (97%)
  local copies, waits for them, and re-layouts  2.39 us (2%)
    pallas_call x1, Pallas kernels, on_device(): pl.pallas_call(kernel, out_shape=(jax.ShapeDtypeStruct((NB, 4, 512), f32)...  131 us

profile of v3, /device:TPU:6, one launch (start us, length us, event | category | flops | bytes accessed | tf_op | source)
XLA Modules:
  0.0 134.5 jit_solution(11932223952473820995)
XLA Ops:
  1.3 130.8 %shard_map.122 = (f32[32,4,512]{2,1,0:T(4,128)}, f32[3,32,512]{2,1,0:T(8,128)}) custom-call(f32[32,4,512]{2,1,0:T(4,128)} %part.1, f32[3,32,512]{2,1,0:T(8,128)} %bitcast.8, f32[10,256]{1,0:T(8,128)} %cells.1, f32[10,64]{1,0:T(8,128)} %top.1, s32[4]{0:T(128)} %act_ids.1, s32[1]{0:T(128)S(6)} %copy.15.act_cnt, s32[4,64]{1,0:T(4,128)} %cell_lists.1, ...), custom_call_target="tpu_custom_call" | custom-call | tf_op jit(solution)/shard_map/pallas_call | solution.py:615
  132.1 0.0 copy-start
  132.1 1.7 %copy.16 = f32[32,4,512]{2,1,0:T(4,128)} copy(f32[32,4,512]{2,1,0:T(4,128)} %get-tuple-element.8) | data formatting | bytes 524288
  133.8 0.0 copy-done
  133.8 0.7 copy.17
Async XLA Ops:
  132.1 1.7 %copy-start = (f32[3,32,512]{2,1,0:T(8,128)S(1)}, f32[3,32,512]{2,1,0:T(8,128)}, u32[]{:S(2)}) copy-start(f32[3,32,512]{2,1,0:T(8,128)} %get-tuple-element.5) | copy-start | bytes 589828

commit v4 on v3

--- a/solution.py
+++ b/solution.py
@@ -61,7 +61,7 @@
     part, vel, cells, top, act_ids, act_cnt, cell_lists, cell_req, leaf_req, leaf_lists, targets,
     outp, outv,
     p_all, v_all, v_y, c_all, t_all, top_m, codes_v, codes_s, l_send,
-    l0, l1, l2, l3, k0, k1, k2, k3, p_rec, pts, acc, own, near,
+    l0, l1, l2, l3, k0, k1, k2, k3, p_rec, pts, acc, own, chosen, picks, near,
     p_ss, p_rs, c_ss, c_rs, v_ss, v_rs, t_ss, t_rs, d_ss, d_rs, vy_ss, vy_rs,
     cy_ss, cy_rs, l_ss, l_rs, pr_ss, pr_rs, kz_ss, kz_rs, ky_ss, ky_rs, loc,
 ):
@@ -85,11 +85,16 @@
     own_v = pltpu.make_async_copy(vel, v_y.at[pl.ds(y * 3, 3)], loc.at[1])
     own_p.start()
     own_v.start()
-    c_all[bulk, pl.ds(0, 8), :] = cells[pl.ds(0, 8), :]
-    c_all[bulk, pl.ds(8, 8), :] = jnp.concatenate(
-        [cells[pl.ds(8, 2), :]]
-        + [jnp.full((1, 256), ident_of(a), jnp.float32) for a in range(ACT)]
-        + [jnp.zeros((2, 256), jnp.float32)],
+    tall = jnp.transpose(
+        jnp.concatenate([cells[...], jnp.zeros((128 - 10, 256), jnp.float32)], axis=0)
+    )
+    packed = tall[0:32]
+    for g in range(1, 8):
+        packed = packed + pltpu.roll(tall[32 * g : 32 * g + 32], 16 * g, 1)
+    c_all[bulk, pl.ds(0, 32), :] = packed
+    c_all[bulk, pl.ds(32, 8), :] = jnp.concatenate(
+        [jnp.full((1, 128), ident_of(a), jnp.float32) for a in range(ACT)]
+        + [jnp.zeros((4, 128), jnp.float32)],
         axis=0,
     )
     t_all[leaf] = jnp.zeros((16, 128), jnp.float32)
@@ -114,13 +119,13 @@
     def greet(dev):
         pl.semaphore_signal(barrier, inc=1, device_id=dev, device_id_type=MESH)
 
-    for d in (1, 2, 4, 8, NZ - 4, NZ - 2, NZ - 1):
+    for d in (1, NZ - 1):
         greet({"bulk": row_peer(d)})
     for d in range(1, NY):
         greet({"bulk": col_peer(d)})
     for d in range(1, NL):
         greet({"leaf": (leaf + d) % NL})
-    pl.semaphore_wait(barrier, 7 + NY + NL - 2)
+    pl.semaphore_wait(barrier, 2 + NY + NL - 2)
 
     def remote(src, dst, ss, rs, dev):
         return pltpu.make_async_remote_copy(
@@ -199,6 +204,10 @@
         for hop in close:
             kz_copy(a, hop).start()
 
+    def k_row(a):
+        for hop in range(1, NZ):
+            kz_copy(a, (NZ // 2 + hop * (hop % 2 * 2 - 1) // 2) % NZ).start()
+
     def k_close(a):
         for base in far:
             kz_copy(a, base).wait_recv()
@@ -206,9 +215,9 @@
                 kz_copy(a, hop, base).start()
 
     def y_send(a):
-        for base in (0,) + far:
-            for hop in close:
-                kz_copy(a, hop, base).wait_recv()
+        for dist in range(1, NZ):
+            if a == ACT - 1 or dist not in far:
+                kz_copy(a, dist).wait_recv()
         for d in (2, 1, 3):
             ky_copy(a, d).start()
 
@@ -329,26 +338,21 @@
                 def _():
                     c_copy(way, i + 1).start()
 
-    def first_events(i, _):
-        c_event(i)
+    def more_events(i, _):
         p_event(i)
+
+        @pl.when((i % 2 == 1) & (i < 16))
+        def _():
+            c_event(i // 2)
+
         self_top(i // 8, (i % 8) * 8, 8)
         return 0
 
-    lax.fori_loop(0, 8, first_events, 0)
+    lax.fori_loop(0, 8, more_events, 0)
     y_forward(vy_copy)
-    for k in range(2):
-        cy_copy(k).start()
-
-    def more_events(i, _):
-        p_event(i)
-        self_top(i // 8, (i % 8) * 8, 8)
-        return 0
-
     lax.fori_loop(8, 16, more_events, 0)
 
     y_done(vy_copy)
-    y_forward(cy_copy)
 
     def pick_row(j, _):
         shift = (targets[j] - bulk) & 63
@@ -359,31 +363,12 @@
         return 0
 
     lax.fori_loop(0, NB, pick_row, 0, unroll=8)
+    for k in range(2):
+        cy_copy(k).start()
     lax.fori_loop(16, 24, more_events, 0)
 
-    y_done(cy_copy)
-    lane16 = lax.broadcasted_iota(jnp.int32, (16, 128), 1)
-    lane256 = lax.broadcasted_iota(jnp.int32, (16, 256), 1)
-    for part_at in range(2):
-
-        def pick_cell(i, got, part_at=part_at):
-            f = cell_lists[part_at * 2 + i // CPER, i % CPER]
-            peer = f >> 4
-            col = cell_req[f & 15, peer] & 255
-            one = jnp.where(lane256 == col, c_all[peer], 0.0)
-            return jnp.where(lane16 == i, jnp.sum(one, axis=1, keepdims=True), got)
-
-        near[:, pl.ds(part_at * 128, 128)] = lax.fori_loop(
-            0, 128, pick_cell, jnp.zeros((16, 128), jnp.float32), unroll=8
-        )
-
-    def last_events(i, _):
-        p_event(i)
-        self_top(i // 8, (i % 8) * 8, 8)
-        near_part((i - 24) // 2, (i % 2) * (OCT // 2), OCT // 2)
-        return 0
-
-    lax.fori_loop(24, 32, last_events, 0)
+    y_forward(cy_copy)
+    lax.fori_loop(24, 32, more_events, 0)
 
     own_p.wait()
     for d in range(1, NY):
@@ -392,6 +377,10 @@
     codes_copy.start()
     codes_copy.wait()
 
+    for way in range(2):
+        for sub in range(3):
+            v_copy(way, 0, sub).start()
+
     def leaf_at(number):
         return p_all[(number >> 5) & 15, number & 31]
 
@@ -411,10 +400,6 @@
             return 0
 
         lax.fori_loop(0, LPER, fill_own, 0, unroll=True)
-
-    for way in range(2):
-        for sub in range(3):
-            v_copy(way, 0, sub).start()
 
     def pick_moved(j, _):
         from_z = (bulk - (targets[j] - bulk)) & 15
@@ -424,6 +409,26 @@
     lax.fori_loop(0, NB, pick_moved, 0, unroll=8)
     for k in range(2):
         pr_copy(k).start()
+
+    y_done(cy_copy)
+
+    def pick_cell(i, _):
+        f = cell_lists[i // CPER, i % CPER]
+        peer = f >> 4
+        col = cell_req[f & 15, peer] & 255
+        chosen[pl.ds(i, 1), :] = c_all[peer, pl.ds(col & 31, 1), :]
+        picks[pl.ds(i, 1), :] = jnp.full((1, 128), col >> 5, jnp.int32)
+        return 0
+
+    lax.fori_loop(0, ACT * CPER, pick_cell, 0, unroll=8)
+    got = chosen[...]
+    group = picks[...]
+    one = jnp.where(group == 0, got, 0.0)
+    for g in range(1, 8):
+        one = jnp.where(group == g, pltpu.roll(got, 128 - 16 * g, 1), one)
+    near[...] = jnp.transpose(one)
+    for a in range(ACT):
+        near_part(a, 0, OCT)
 
     def v_event(i):
         h = i // 3
@@ -495,7 +500,10 @@
                 k_all[a][bulk, pl.ds(row, 1), pl.ds(col * 128, 128)] = pull[
                     :, b * 128 : (b + 1) * 128
                 ]
-        k_far(a)
+        if a < ACT - 1:
+            k_far(a)
+        else:
+            k_row(a)
 
     def v_events(lo, hi):
         def go(i, _):
@@ -538,7 +546,6 @@
             l_copy(a, d).wait_send()
     v_events(18, 19)
     y_send(2)
-    k_close(3)
     v_events(19, 21)
     y_done(pr_copy)
     for k in range(4):
@@ -571,7 +578,7 @@
         from_y = source >> 4
         from_z = source & 15
         number = j.astype(jnp.float32)
-        hits = [c_all[source, pl.ds(10 + a, 1), pl.ds(0, 128)] == number for a in range(ACT)]
+        hits = [c_all[source, pl.ds(32 + a, 1), :] == number for a in range(ACT)]
         for c in range(3):
             parts = []
             for b in range(4):
@@ -624,7 +631,7 @@
             pltpu.VMEM((NZ, NB, 4, 512), f32),
             pltpu.VMEM((NZ, 3, NB, 512), f32),
             pltpu.VMEM((NY * 3, NB, 512), f32),
-            pltpu.VMEM((NY * NZ, 16, 256), f32),
+            pltpu.VMEM((NY * NZ, 40, 128), f32),
             pltpu.VMEM((NL, 16, 128), f32),
             pltpu.VMEM((16, 512), f32),
             pltpu.VMEM((NY, 8, 128), jnp.int32),
@@ -638,7 +645,9 @@
             pltpu.VMEM((ACT, 3, 512, 128), f32),
             pltpu.VMEM((ACT, 3, 512, 128), f32),
             pltpu.VMEM((ACT, 8, 512), f32),
-            pltpu.VMEM((16, ACT * CPER), f32),
+            pltpu.VMEM((ACT * CPER, 128), f32),
+            pltpu.VMEM((ACT * CPER, 128), jnp.int32),
+            pltpu.VMEM((128, ACT * CPER), f32),
             dma((2, 8, SUBS)),
             dma((2, 8, SUBS)),
             dma((2, 8)),

time: 135 us -> 129 us (0.956)
  Pallas kernels: 131 us -> 124 us
    pallas_call x1, Pallas kernels: 131 us -> 124 us  [on_device(): pl.pallas_call(kernel, out_shape=(jax.ShapeDtypeStruct((NB, 4, 512), f32)...]
where the time goes in v4:
time: 129 us; the launch traced here: 128 us
  Pallas kernels  124 us (96%)
  local copies, waits for them, and re-layouts  2.39 us (2%)
  between operations  1.3 us (1%)
    pallas_call x1, Pallas kernels, on_device(): pl.pallas_call(kernel, out_shape=(jax.ShapeDtypeStruct((NB, 4, 512), f32)...  124 us

profile of v4, /device:TPU:6, one launch (start us, length us, event | category | flops | bytes accessed | tf_op | source)
XLA Modules:
  0.0 127.8 jit_solution(17802580640001941671)
XLA Ops:
  1.3 124.1 %shard_map.122 = (f32[32,4,512]{2,1,0:T(4,128)}, f32[3,32,512]{2,1,0:T(8,128)}) custom-call(f32[32,4,512]{2,1,0:T(4,128)} %part.1, f32[3,32,512]{2,1,0:T(8,128)} %bitcast.8, f32[10,256]{1,0:T(8,128)} %cells.1, f32[10,64]{1,0:T(8,128)} %top.1, s32[4]{0:T(128)} %act_ids.1, s32[1]{0:T(128)S(6)} %copy.15.act_cnt, s32[4,64]{1,0:T(4,128)} %cell_lists.1, ...), custom_call_target="tpu_custom_call" | custom-call | tf_op jit(solution)/shard_map/pallas_call | solution.py:622
  125.4 0.0 copy-start
  125.4 1.7 %copy.16 = f32[32,4,512]{2,1,0:T(4,128)} copy(f32[32,4,512]{2,1,0:T(4,128)} %get-tuple-element.8) | data formatting | bytes 524288
  127.1 0.0 copy-done
  127.1 0.7 copy.17
Async XLA Ops:
  125.4 1.7 %copy-start = (f32[3,32,512]{2,1,0:T(8,128)S(1)}, f32[3,32,512]{2,1,0:T(8,128)}, u32[]{:S(2)}) copy-start(f32[3,32,512]{2,1,0:T(8,128)} %get-tuple-element.5) | copy-start | bytes 589828

commit v5 on v4

--- a/solution.py
+++ b/solution.py
@@ -20,6 +20,13 @@
 SUBS = 4
 SROW = NB // SUBS
 OCT = 64
+V_CAP = [NB] + [min(NB - 2, 8 * (8 - h) + 4) for h in range(1, 9)]
+V_PLAN = (
+    ((1, 0), (3, 1), (5, 2)),
+    ((0, 3), (1, 4), (3, 5), (5, 6)),
+    ((0, 7), (1, 8), (3, 9), (5, 10)),
+    ((0, 11), (1, 12), (3, 13), (5, 14)),
+)
 
 
 def pair_terms(px, py, pz, src, accs):
@@ -60,7 +67,7 @@
 def kernel(
     part, vel, cells, top, act_ids, act_cnt, cell_lists, cell_req, leaf_req, leaf_lists, targets,
     outp, outv,
-    p_all, v_all, v_y, c_all, t_all, top_m, codes_v, codes_s, l_send,
+    p_all, v_rg, tab_v, tab_s, v_y, c_all, t_all, top_m, codes_v, codes_s, l_send,
     l0, l1, l2, l3, k0, k1, k2, k3, p_rec, pts, acc, own, chosen, picks, near,
     p_ss, p_rs, c_ss, c_rs, v_ss, v_rs, t_ss, t_rs, d_ss, d_rs, vy_ss, vy_rs,
     cy_ss, cy_rs, l_ss, l_rs, pr_ss, pr_rs, kz_ss, kz_rs, ky_ss, ky_rs, loc,
@@ -149,9 +156,15 @@
         at = c_all.at[y * NZ + ring_src(way, h)]
         return remote(at, at, c_ss.at[way, h], c_rs.at[way, h], ring_dev(way))
 
+    def v_cut(h, sub):
+        lo, hi = sub * 10, min(sub * 10 + 10, V_CAP[h])
+        return lo, hi - lo
+
     def v_copy(way, h, sub):
-        at = v_all.at[ring_src(way, h), sub]
-        return remote(at, at, v_ss.at[way, h, sub], v_rs.at[way, h, sub], ring_dev(way))
+        lo, size = v_cut(h, sub)
+        src = v_rg.at[pl.ds((way * 9 + h - 1) * NB + lo, size)]
+        dst = v_rg.at[pl.ds((way * 9 + h) * NB + lo, size)]
+        return remote(src, dst, v_ss.at[way, h, sub], v_rs.at[way, h, sub], ring_dev(way))
 
     def t_copy(d):
         return remote(t_all.at[leaf], t_all.at[leaf], t_ss.at[d], t_rs.at[d], {"leaf": (leaf + d) % NL})
@@ -244,6 +257,48 @@
     for k in range(2):
         vy_copy(k).start()
 
+    row32 = lax.broadcasted_iota(jnp.int32, (32, 128), 0)
+    offs = [(targets[j] - bulk) & 15 for j in range(NB)]
+    off_col = jnp.zeros((32, 128), jnp.int32)
+    off_row = jnp.zeros((8, 128), jnp.int32)
+    for j in range(NB):
+        off_col = jnp.where(row32 == j, offs[j], off_col)
+        off_row = jnp.where(lanes == j, offs[j], off_row)
+    half_col = jnp.zeros((32, 128), jnp.int32)
+    half_row = jnp.zeros((8, 128), jnp.int32)
+    for j in range(NB):
+        half_col = half_col + jnp.where((offs[j] == 8) & (row32 > j), 1, 0)
+        half_row = half_row + jnp.where((offs[j] == 8) & (lanes > j), 1, 0)
+
+    def split(off, half):
+        back = (off > 8) | ((off == 8) & (half >= 4))
+        return jnp.where(back, 0, off), jnp.where(back, 16 - off, 0)
+
+    dist_col = split(off_col, half_col)
+    dist_row = split(off_row, half_row)
+    table = jnp.zeros((8, 128), jnp.int32)
+    code = jnp.zeros((8, 128), jnp.int32)
+    for way in range(2):
+        place_col = jnp.zeros((32, 128), jnp.int32)
+        place_row = jnp.zeros((8, 128), jnp.int32)
+        for j in range(NB):
+            mine = dist_col[way][j : j + 1, :]
+            place_col = place_col + jnp.where(
+                (mine > dist_col[way]) | ((mine == dist_col[way]) & (row32 > j)), 1, 0
+            )
+            place_row = place_row + jnp.where(
+                (mine > dist_row[way]) | ((mine == dist_row[way]) & (lanes > j)), 1, 0
+            )
+        held = jnp.zeros((8, 128), jnp.int32)
+        for j in range(NB):
+            held = jnp.where(place_col[j : j + 1, :] == lanes, j, held)
+        table = jnp.where(rows == way, held, table)
+        spot = (way * 9 + dist_row[way]) * NB + place_row
+        code = spot if way == 0 else jnp.where(dist_row[1] > 0, spot, code)
+    tab_v[...] = jnp.where(rows == 2, code, table)
+    tab_copy = pltpu.make_async_copy(tab_v, tab_s, loc.at[3])
+    tab_copy.start()
+
     for a in range(ACT):
         bucket = part[act_ids[a]]
         own[a, pl.ds(0, 4), :] = bucket
@@ -354,15 +409,24 @@
 
     y_done(vy_copy)
 
-    def pick_row(j, _):
-        shift = (targets[j] - bulk) & 63
-        to_z = (z + shift) & 15
-        from_y = ((y * NZ + to_z - shift) & 63) >> 4
-        for c in range(3):
-            v_all[z, c, pl.ds(j, 1), :] = v_y[from_y * 3 + c, pl.ds(j, 1), :]
-        return 0
-
-    lax.fori_loop(0, NB, pick_row, 0, unroll=8)
+    tab_copy.wait()
+    for way in range(2):
+
+        def pick_row(slot, _, way=way):
+            j = tab_s[way, slot] & 31
+            shift = (targets[j] - bulk) & 63
+            to_z = (z + shift) & 15
+            from_y = ((y * NZ + to_z - shift) & 63) >> 4
+            for c in range(3):
+                line = v_y[from_y * 3 + c, pl.ds(j, 1), :]
+                for b in range(4):
+                    row, col = divmod(c * 4 + b, 3)
+                    v_rg[way * 9 * NB + slot, pl.ds(row, 1), pl.ds(col * 128, 128)] = line[
+                        :, b * 128 : (b + 1) * 128
+                    ]
+            return 0
+
+        lax.fori_loop(0, NB, pick_row, 0, unroll=4)
     for k in range(2):
         cy_copy(k).start()
     lax.fori_loop(16, 24, more_events, 0)
@@ -379,7 +443,7 @@
 
     for way in range(2):
         for sub in range(3):
-            v_copy(way, 0, sub).start()
+            v_copy(way, 1, sub).start()
 
     def leaf_at(number):
         return p_all[(number >> 5) & 15, number & 31]
@@ -430,19 +494,18 @@
     for a in range(ACT):
         near_part(a, 0, OCT)
 
+    hops = [(h, sub) for h in range(1, 9) for sub in range(3) if V_CAP[h] > sub * 10]
+
     def v_event(i):
-        h = i // 3
-        sub = i % 3
+        h, sub = hops[i]
         for way in range(2):
-            mine = (sub == 0) if way == 0 else (sub > 0)
-
-            @pl.when((h < NZ // 2 - 1) | mine)
-            def _():
-                v_copy(way, h, sub).wait_recv()
-
-            @pl.when((h < NZ // 2 - 2) | ((h == NZ // 2 - 2) & mine))
-            def _():
+            v_copy(way, h, sub).wait_recv()
+            if (h + 1, sub) in hops:
                 v_copy(way, h + 1, sub).start()
+
+    def v_events(lo, hi):
+        for i in range(lo, hi):
+            v_event(i)
 
     for a in range(ACT):
         for d in range(1, NY):
@@ -465,17 +528,11 @@
 
             lax.fori_loop(0, OCT, step, 0, unroll=8)
 
-            first = a * 4 - (a > 0)
-
-            @pl.when(e % 2 == 1)
-            def _():
-                v_event(first + (a > 0) + e // 2)
-
-            if a > 0:
-
-                @pl.when(e == 0)
-                def _():
-                    v_event(first)
+            for at, number in V_PLAN[a]:
+
+                @pl.when(e == at)
+                def _(number=number):
+                    v_event(number)
 
             if a >= 2:
 
@@ -505,13 +562,6 @@
         else:
             k_row(a)
 
-    def v_events(lo, hi):
-        def go(i, _):
-            v_event(i)
-            return 0
-
-        lax.fori_loop(lo, hi, go, 0)
-
     for d in range(1, NL):
         t_copy(d).wait_send()
 
@@ -528,11 +578,10 @@
         return 0
 
     lax.fori_loop(0, 32, p_sent, 0)
+    y_send(1)
     v_events(15, 16)
-    y_send(1)
+    k_close(2)
     v_events(16, 17)
-    k_close(2)
-    v_events(17, 18)
     for h in range(NZ // 2):
         c_copy(0, h).wait_send()
         if h < NZ // 2 - 1:
@@ -544,28 +593,16 @@
         d_copy(d).wait_send()
         for a in range(ACT):
             l_copy(a, d).wait_send()
-    v_events(18, 19)
     y_send(2)
-    v_events(19, 21)
+    v_events(17, 18)
     y_done(pr_copy)
     for k in range(4):
         pr_copy(k).wait_send()
     y_send(3)
-    v_events(21, 24)
-
-    def v_sent(i, _):
-        h = i // 3
-        sub = i % 3
+    v_events(18, 20)
+    for h, sub in hops:
         for way in range(2):
-            mine = (sub == 0) if way == 0 else (sub > 0)
-
-            @pl.when((h < NZ // 2 - 1) | mine)
-            def _():
-                v_copy(way, h, sub).wait_send()
-
-        return 0
-
-    lax.fori_loop(0, 24, v_sent, 0)
+            v_copy(way, h, sub).wait_send()
     for a in range(ACT):
         for dist in range(1, NZ):
             kz_copy(a, dist).wait_send()
@@ -576,19 +613,20 @@
     def place(j, _):
         source = (bulk - (targets[j] - bulk)) & 63
         from_y = source >> 4
-        from_z = source & 15
+        spot_j = tab_s[2, j]
         number = j.astype(jnp.float32)
         hits = [c_all[source, pl.ds(32 + a, 1), :] == number for a in range(ACT)]
         for c in range(3):
             parts = []
             for b in range(4):
                 row, col = divmod(c * 4 + b, 3)
+                cut = pl.ds(col * 128, 128)
                 kick = jnp.zeros((1, 128), jnp.float32)
                 for a in range(ACT):
-                    got = k_all[a][source, pl.ds(row, 1), pl.ds(col * 128, 128)]
+                    got = k_all[a][source, pl.ds(row, 1), cut]
                     kick = kick + jnp.where(hits[a], got, 0.0)
-                parts.append(kick)
-            speed = v_all[from_z, c, pl.ds(j, 1), :] + jnp.concatenate(parts, axis=1)
+                parts.append(v_rg[spot_j, pl.ds(row, 1), cut] + kick)
+            speed = jnp.concatenate(parts, axis=1)
             outv[c, pl.ds(j, 1), :] = speed
             outp[j, pl.ds(c, 1), :] = p_rec[from_y * NB + j, pl.ds(c, 1), :] + step_time * speed
         outp[j, pl.ds(3, 1), :] = p_rec[from_y * NB + j, pl.ds(3, 1), :]
@@ -629,7 +667,9 @@
         out_specs=(vmem, vmem),
         scratch_shapes=[
             pltpu.VMEM((NZ, NB, 4, 512), f32),
-            pltpu.VMEM((NZ, 3, NB, 512), f32),
+            pltpu.VMEM((2 * 9 * NB, 4, 384), f32),
+            pltpu.VMEM((8, 128), jnp.int32),
+            pltpu.SMEM((8, 128), jnp.int32),
             pltpu.VMEM((NY * 3, NB, 512), f32),
             pltpu.VMEM((NY * NZ, 40, 128), f32),
             pltpu.VMEM((NL, 16, 128), f32),
@@ -652,8 +692,8 @@
             dma((2, 8, SUBS)),
             dma((2, 8)),
             dma((2, 8)),
-            dma((2, 8, 3)),
-            dma((2, 8, 3)),
+            dma((2, 9, 3)),
+            dma((2, 9, 3)),
             dma((NL,)),
             dma((NL,)),
             dma((NY,)),

time: 129 us -> 126 us (0.977)
  Pallas kernels: 124 us -> 122 us
    pallas_call x1, Pallas kernels: 124 us -> 122 us  [on_device(): pl.pallas_call(kernel, out_shape=(jax.ShapeDtypeStruct((NB, 4, 512), f32)...]
where the time goes in v5:
time: 126 us
  Pallas kernels  122 us (97%)
  local copies, waits for them, and re-layouts  2.39 us (2%)
  between operations  1.3 us (1%)
    pallas_call x1, Pallas kernels, on_device(): pl.pallas_call(kernel, out_shape=(jax.ShapeDtypeStruct((NB, 4, 512), f32)...  122 us

profile of v5, /device:TPU:6, one launch (start us, length us, event | category | flops | bytes accessed | tf_op | source)
XLA Modules:
  0.0 125.9 jit_solution(8984133912243765027)
XLA Ops:
  1.3 122.2 %shard_map.122 = (f32[32,4,512]{2,1,0:T(4,128)}, f32[3,32,512]{2,1,0:T(8,128)}) custom-call(f32[32,4,512]{2,1,0:T(4,128)} %part.1, f32[3,32,512]{2,1,0:T(8,128)} %bitcast.8, f32[10,256]{1,0:T(8,128)} %cells.1, f32[10,64]{1,0:T(8,128)} %top.1, s32[4]{0:T(128)} %act_ids.1, s32[1]{0:T(128)S(6)} %copy.15.act_cnt, s32[4,64]{1,0:T(4,128)} %cell_lists.1, ...), custom_call_target="tpu_custom_call" | custom-call | tf_op jit(solution)/shard_map/pallas_call | solution.py:660
  123.5 0.0 copy-start
  123.5 1.7 %copy.16 = f32[32,4,512]{2,1,0:T(4,128)} copy(f32[32,4,512]{2,1,0:T(4,128)} %get-tuple-element.8) | data formatting | bytes 524288
  125.2 0.0 copy-done
  125.2 0.7 copy.17
Async XLA Ops:
  123.5 1.7 %copy-start = (f32[3,32,512]{2,1,0:T(8,128)S(1)}, f32[3,32,512]{2,1,0:T(8,128)}, u32[]{:S(2)}) copy-start(f32[3,32,512]{2,1,0:T(8,128)} %get-tuple-element.5) | copy-start | bytes 589828

commit v6 on v5

--- a/solution.py
+++ b/solution.py
@@ -22,10 +22,10 @@
 OCT = 64
 V_CAP = [NB] + [min(NB - 2, 8 * (8 - h) + 4) for h in range(1, 9)]
 V_PLAN = (
-    ((1, 0), (3, 1), (5, 2)),
-    ((0, 3), (1, 4), (3, 5), (5, 6)),
-    ((0, 7), (1, 8), (3, 9), (5, 10)),
-    ((0, 11), (1, 12), (3, 13), (5, 14)),
+    ((0, 0), (1, 1), (3, 2), (5, 3)),
+    ((0, 4), (1, 5), (3, 6), (5, 7)),
+    ((0, 8), (1, 9), (3, 10), (5, 11)),
+    ((0, 12), (1, 13), (3, 14), (5, 15)),
 )
 
 
@@ -579,7 +579,6 @@
 
     lax.fori_loop(0, 32, p_sent, 0)
     y_send(1)
-    v_events(15, 16)
     k_close(2)
     v_events(16, 17)
     for h in range(NZ // 2):

time: 126 us -> 124 us (0.984)
  Pallas kernels: 122 us -> 120 us
    pallas_call x1, Pallas kernels: 122 us -> 120 us  [on_device(): pl.pallas_call(kernel, out_shape=(jax.ShapeDtypeStruct((NB, 4, 512), f32)...]
where the time goes in v6:
time: 124 us
  Pallas kernels  120 us (97%)
  local copies, waits for them, and re-layouts  2.39 us (2%)
  between operations  1.3 us (1%)
    pallas_call x1, Pallas kernels, on_device(): pl.pallas_call(kernel, out_shape=(jax.ShapeDtypeStruct((NB, 4, 512), f32)...  120 us

profile of v6, /device:TPU:6, one launch (start us, length us, event | category | flops | bytes accessed | tf_op | source)
XLA Modules:
  0.0 124.0 jit_solution(5378709639361032831)
XLA Ops:
  1.3 120.3 %shard_map.122 = (f32[32,4,512]{2,1,0:T(4,128)}, f32[3,32,512]{2,1,0:T(8,128)}) custom-call(f32[32,4,512]{2,1,0:T(4,128)} %part.1, f32[3,32,512]{2,1,0:T(8,128)} %bitcast.8, f32[10,256]{1,0:T(8,128)} %cells.1, f32[10,64]{1,0:T(8,128)} %top.1, s32[4]{0:T(128)} %act_ids.1, s32[1]{0:T(128)S(6)} %copy.15.act_cnt, s32[4,64]{1,0:T(4,128)} %cell_lists.1, ...), custom_call_target="tpu_custom_call" | custom-call | tf_op jit(solution)/shard_map/pallas_call | solution.py:659
  121.6 0.0 copy-start
  121.6 1.7 %copy.16 = f32[32,4,512]{2,1,0:T(4,128)} copy(f32[32,4,512]{2,1,0:T(4,128)} %get-tuple-element.8) | data formatting | bytes 524288
  123.3 0.0 copy-done
  123.3 0.7 copy.17
Async XLA Ops:
  121.6 1.7 %copy-start = (f32[3,32,512]{2,1,0:T(8,128)S(1)}, f32[3,32,512]{2,1,0:T(8,128)}, u32[]{:S(2)}) copy-start(f32[3,32,512]{2,1,0:T(8,128)} %get-tuple-element.5) | copy-start | bytes 589828
